TPU v7x, 32 devices: a whole 2x2x4 slice. The times are simulated.
32 devices in a mesh: dp: 8 (over y, x, core), seq: 4 (over z).
Axes of the slice: x: 2, y: 2, z: 4, core: 2. Of those that a mesh axis runs over, the one named last changes fastest.
Arguments:
- hidden_in: bfloat16 [32, 512, 768], P('dp', 'seq'), may hold values from -6 to 6
- query_lengths: int32 [32], P('dp'), may hold values from 1 to 64, as said below
- doc_lengths: int32 [32], P('dp'), may hold values from 32 to 448, as said below
- w_query: bfloat16 [768, 768], replicated, may hold values from -0.109375 to 0.109375
- w_key: bfloat16 [768, 768], replicated, may hold values from -0.109375 to 0.109375
- w_value: bfloat16 [768, 768], replicated, may hold values from -0.21875 to 0.21875
- w_attn_out: bfloat16 [768, 768], replicated, may hold values from -0.875 to 0.875
- w_inner: bfloat16 [768, 3072], replicated, may hold values from -0.21875 to 0.21875
- w_outer: bfloat16 [3072, 768], replicated, may hold values from -0.109375 to 0.109375
- gain_attn: bfloat16 [768], replicated, may hold values from 0.5 to 1.5
- gain_ffn: bfloat16 [768], replicated, may hold values from 0.5 to 1.5
- bias_table: bfloat16 [32, 12], replicated, may hold values from -4 to 4
- cotangent: bfloat16 [32, 512, 768], P('dp', 'seq'), may hold values from -6 to 6
Outputs:
- layer_out: bfloat16 [32, 512, 768], P('dp', 'seq')
- grad_in: bfloat16 [32, 512, 768], P('dp', 'seq')
- grad_query: float32 [768, 768], P('dp')
- grad_key: float32 [768, 768], P('dp')
- grad_value: float32 [768, 768], P('dp')
- grad_attn_out: float32 [768, 768], P('dp')
- grad_inner: float32 [768, 3072], P('dp')
- grad_outer: float32 [3072, 768], P('dp')
- grad_gain_attn: float32 [768], P('dp')
- grad_gain_ffn: float32 [768], P('dp')
- grad_table: float32 [32, 12], replicated
Inputs may be any that keep to these rules, and one draw needn't show every extreme that they name: `query_lengths`: in each aligned block of 2 rows one row has exactly 64 query tokens and fills all 512 slots. `doc_lengths`: A row's query and document tokens together take at most 512 slots; its other slots are padding. The row that fills all 512 slots has exactly 448 document tokens.
All inputs are finite; a program needn't handle non-finite values.
Results may differ from a plain program's by a relative error of at most 0.018.
Values may be sent and summed in bfloat16 or wider, within the bound.
A program may use at most 256 MiB of HBM per device.

v0:
```python
from functools import partial

import jax
import jax.numpy as jnp
from jax import lax
from jax.sharding import PartitionSpec as P

ROWS_DEV = 2


EPS = 1e-06
NEG = -1000000000.0
LIMITS = (12, 16, 23, 32, 46, 64, 91)
HIGH = lax.Precision.HIGHEST


def shortened(array):

    def short(part):
        return part.astype(jnp.bfloat16) if part.dtype == jnp.float32 else part

    return jax.tree.map(short, array)


def rms_scale(values, gain_vec):
    factor = lax.rsqrt(jnp.mean(values * values, axis=-1, keepdims=True) + EPS)
    return values * factor * gain_vec


def buckets(relative):
    distance = jnp.abs(relative)
    far_bucket = 8 + sum(((distance >= thresh).astype(jnp.int32) for thresh in LIMITS))
    return jnp.where(relative > 0, 16, 0) + jnp.where(distance < 8, distance, far_bucket)


def position_bias(table_f, query_pos, key_pos):
    relative = key_pos[None, :] - query_pos[:, None]
    bucket_count, head_count = table_f.shape
    one_hot = (buckets(relative)[:, :, None] == jnp.arange(bucket_count)[None, None, :]).astype(
        jnp.float32
    )
    one_hot = one_hot.reshape(query_pos.shape[0] * key_pos.shape[0], bucket_count)
    pos_bias = jnp.dot(one_hot, table_f, precision=HIGH).reshape(
        query_pos.shape[0], key_pos.shape[0], head_count
    )
    return (one_hot, pos_bias.transpose(2, 0, 1))


def split_heads(arr, head_count):
    return arr.reshape(arr.shape[0], arr.shape[1], head_count, arr.shape[2] // head_count)


def scores_of(query_rows, key_rows, pos_bias, key_live):
    head_count = pos_bias.shape[0]
    scores = jnp.einsum(
        "rqhd,rkhd->rhqk",
        split_heads(query_rows, head_count),
        split_heads(key_rows, head_count),
        preferred_element_type=jnp.float32,
    )
    scores = scores + pos_bias[None]
    return jnp.where(key_live[:, None, None, :], scores, NEG)


def outer_sum(left, right):
    return lax.dot_general(
        left, right, (((0,), (0,)), ((), ())), preferred_element_type=jnp.float32
    )


def back_dot(grad_rows, weight):
    return lax.dot_general(
        grad_rows, weight, (((1,), (1,)), ((), ())), preferred_element_type=jnp.float32
    )


def on_device(
    hidden_in,
    query_lengths,
    doc_lengths,
    w_query,
    w_key,
    w_value,
    w_attn_out,
    w_inner,
    w_outer,
    gain_attn,
    gain_ffn,
    bias_table,
    cotangent,
):
    all_rows, block_len, width = hidden_in.shape
    row_count = ROWS_DEV
    batches = all_rows // row_count
    head_count = bias_table.shape[1]
    tokens = row_count * block_len
    gain_one = gain_attn.astype(jnp.float32)
    gain_two = gain_ffn.astype(jnp.float32)
    table_f = bias_table.astype(jnp.float32)
    block_start = lax.axis_index("seq") * block_len

    def micro_step(totals, inputs):
        hidden_part, cot_part, query_part, doc_part = inputs
        resid_in = hidden_part.astype(jnp.float32).reshape(tokens, width)
        normed_one = rms_scale(resid_in, gain_one).astype(jnp.bfloat16)
        query_low = jnp.dot(normed_one, w_query, preferred_element_type=jnp.float32).astype(
            jnp.bfloat16
        )
        key_low = jnp.dot(normed_one, w_key, preferred_element_type=jnp.float32).astype(
            jnp.bfloat16
        )
        value_low = jnp.dot(normed_one, w_value, preferred_element_type=jnp.float32).astype(
            jnp.bfloat16
        )
        query_three = query_low.reshape(row_count, block_len, width)
        key_three = key_low.reshape(row_count, block_len, width)
        value_three = value_low.reshape(row_count, block_len, width)
        all_keys, all_values = (
            lax.all_gather(key_three, "seq", axis=1, tiled=True),
            lax.all_gather(value_three, "seq", axis=1, tiled=True),
        )
        length = all_keys.shape[1]
        total_len = query_part + doc_part
        query_pos = block_start + jnp.arange(block_len)
        key_pos = jnp.arange(length)
        key_live = key_pos[None, :] < total_len[:, None]
        one_hot, pos_bias = position_bias(table_f, query_pos, key_pos)
        scores = scores_of(query_three, all_keys, pos_bias, key_live)
        row_max = jnp.max(scores, axis=-1, keepdims=True)
        exponent = jnp.exp(scores - row_max)
        row_total = jnp.sum(exponent, axis=-1, keepdims=True)
        probs = exponent / row_total
        log_total = (row_max + jnp.log(row_total))[..., 0]
        value_heads = split_heads(all_values, head_count)
        attended = jnp.einsum(
            "rhqk,rkhd->rqhd",
            probs.astype(jnp.bfloat16),
            value_heads,
            preferred_element_type=jnp.float32,
        )
        attended_low = attended.reshape(tokens, width).astype(jnp.bfloat16)
        resid_mid = resid_in + jnp.dot(attended_low, w_attn_out, preferred_element_type=jnp.float32)
        normed_two = rms_scale(resid_mid, gain_two).astype(jnp.bfloat16)
        inner = jnp.dot(normed_two, w_inner, preferred_element_type=jnp.float32)
        active = jax.nn.gelu(inner, approximate=True).astype(jnp.bfloat16)
        layer_part = (
            resid_mid + jnp.dot(active, w_outer, preferred_element_type=jnp.float32)
        ).astype(jnp.bfloat16)
        cot_flat = cot_part.reshape(tokens, width)
        grad_outer_w = outer_sum(active, cot_flat)
        grad_active = back_dot(cot_flat, w_outer)
        gelu_out, gelu_back = jax.vjp(partial(jax.nn.gelu, approximate=True), inner)
        grad_inner_low = gelu_back(grad_active)[0].astype(jnp.bfloat16)
        grad_inner_w = outer_sum(normed_two, grad_inner_low)
        grad_normed_two = back_dot(grad_inner_low, w_inner)
        norm_out, norm_two_back = jax.vjp(rms_scale, resid_mid, gain_two)
        grad_mid_norm, gain_two_grad = norm_two_back(grad_normed_two)
        grad_mid = cot_flat.astype(jnp.float32) + grad_mid_norm
        grad_mid_low = grad_mid.astype(jnp.bfloat16)
        grad_attn_out_w = outer_sum(attended_low, grad_mid_low)
        grad_attended = back_dot(grad_mid_low, w_attn_out).astype(jnp.bfloat16)
        grad_three = grad_attended.reshape(row_count, block_len, width)
        grad_heads = split_heads(grad_three, head_count)
        scores_again = scores_of(query_three, all_keys, pos_bias, key_live)
        probs_again = jnp.exp(scores_again - log_total[..., None])
        grad_prob = jnp.einsum(
            "rqhd,rkhd->rhqk", grad_heads, value_heads, preferred_element_type=jnp.float32
        )
        delta = jnp.sum(probs_again * grad_prob, axis=-1)
        dscore = (probs_again * (grad_prob - delta[..., None])).astype(jnp.bfloat16)
        key_heads = split_heads(all_keys, head_count)
        grad_query_low = (
            jnp.einsum("rhqk,rkhd->rqhd", dscore, key_heads, preferred_element_type=jnp.float32)
            .reshape(tokens, width)
            .astype(jnp.bfloat16)
        )
        score_sum = jnp.sum(dscore, axis=0, dtype=jnp.float32).reshape(
            head_count, block_len * length
        )
        table_grad = lax.dot_general(one_hot, score_sum, (((0,), (1,)), ((), ())), precision=HIGH)
        query_heads = split_heads(query_three, head_count)
        key_terms = jnp.einsum(
            "rhqk,rqhd->rkhd", dscore, query_heads, preferred_element_type=jnp.float32
        ).reshape(row_count, length, width)
        value_terms = jnp.einsum(
            "rhqk,rqhd->rkhd",
            probs_again.astype(jnp.bfloat16),
            grad_heads,
            preferred_element_type=jnp.float32,
        ).reshape(row_count, length, width)
        grad_key_sum, grad_value_sum = (
            lax.psum_scatter(
                key_terms.astype(jnp.bfloat16), "seq", scatter_dimension=1, tiled=True
            ).astype(jnp.float32),
            lax.psum_scatter(
                value_terms.astype(jnp.bfloat16), "seq", scatter_dimension=1, tiled=True
            ).astype(jnp.float32),
        )
        grad_key_low = grad_key_sum.reshape(tokens, width).astype(jnp.bfloat16)
        grad_value_low = grad_value_sum.reshape(tokens, width).astype(jnp.bfloat16)
        grad_query_w = outer_sum(normed_one, grad_query_low)
        grad_key_w = outer_sum(normed_one, grad_key_low)
        grad_value_w = outer_sum(normed_one, grad_value_low)
        grad_normed_one = (
            back_dot(grad_query_low, w_query)
            + back_dot(grad_key_low, w_key)
            + back_dot(grad_value_low, w_value)
        )
        norm_first, norm_one_back = jax.vjp(rms_scale, resid_in, gain_one)
        grad_resid_norm, gain_one_grad = norm_one_back(grad_normed_one)
        grad_part = (
            (grad_mid + grad_resid_norm).astype(jnp.bfloat16).reshape(row_count, block_len, width)
        )
        terms = (
            grad_query_w,
            grad_key_w,
            grad_value_w,
            grad_attn_out_w,
            grad_inner_w,
            grad_outer_w,
            gain_one_grad,
            gain_two_grad,
            table_grad,
        )
        new_totals = tuple((old + add for old, add in zip(totals, terms)))
        return (new_totals, (layer_part.reshape(row_count, block_len, width), grad_part))

    zero_totals = (
        jnp.zeros((width, width), jnp.float32),
        jnp.zeros((width, width), jnp.float32),
        jnp.zeros((width, width), jnp.float32),
        jnp.zeros((width, width), jnp.float32),
        jnp.zeros(w_inner.shape, jnp.float32),
        jnp.zeros(w_outer.shape, jnp.float32),
        jnp.zeros((width,), jnp.float32),
        jnp.zeros((width,), jnp.float32),
        jnp.zeros(bias_table.shape, jnp.float32),
    )
    stacked = (
        hidden_in.reshape(batches, row_count, block_len, width),
        cotangent.reshape(batches, row_count, block_len, width),
        query_lengths.reshape(batches, row_count),
        doc_lengths.reshape(batches, row_count),
    )
    totals, outputs = lax.scan(micro_step, zero_totals, stacked)
    layer_out = outputs[0].reshape(all_rows, block_len, width)
    grad_in = outputs[1].reshape(all_rows, block_len, width)
    local_grads = totals[:8]
    shares = lax.psum_scatter(local_grads, "dp", scatter_dimension=0, tiled=True)
    shares = jax.tree.map(lambda part: part.astype(jnp.float32), lax.psum(shortened(shares), "seq"))
    table_total = lax.psum(totals[8], ("dp", "seq"))
    return (
        layer_out,
        grad_in,
        shares[0],
        shares[1],
        shares[2],
        shares[3],
        shares[4],
        shares[5],
        shares[6],
        shares[7],
        table_total,
    )


def solution(mesh):
    return jax.shard_map(
        on_device,
        mesh=mesh,
        in_specs=(
            P("dp", "seq", None),
            P("dp"),
            P("dp"),
            P(),
            P(),
            P(),
            P(),
            P(),
            P(),
            P(),
            P(),
            P(),
            P("dp", "seq", None),
        ),
        out_specs=(
            P("dp", "seq", None),
            P("dp", "seq", None),
            P("dp", None),
            P("dp", None),
            P("dp", None),
            P("dp", None),
            P("dp", None),
            P("dp", None),
            P("dp"),
            P("dp"),
            P(),
        ),
        check_vma=False,
    )
```

profile of v0, /device:TPU:0, one launch (start us, length us, event | category | flops | bytes accessed | tf_op | source)
XLA Modules:
  0.0 843.7 jit_solution(1221951943012747084)
XLA Ops:
  14.0 390.7 %while.33 = (s32[]{:T(128)}, f32[768,768]{1,0:T(8,128)}, f32[768,768]{1,0:T(8,128)}, f32[768,768]{1,0:T(8,128)}, f32[768,768]{1,0:T(8,128)}, /*index=5*/f32[768,...) while((s32[]{:T(128)}, f32[768,768]{1,0:T(8,128)}, ...), condition=%wide.region_13.14_spmd.clone, body=%wide.region_0.13_spmd.clone.sunk | while | flops 12776308736 | bytes 552435584 | solution.py:245
  34.2 25.4 %all-gather.3.cloned.1.call-done = bf16[2,512,768]{2,1,0:T(8,128)(2,1)} async-done(((bf16[2,128,768]{2,1,0:T(8,128)(2,1)}), bf16[2,512,768]{2,1,0:T(8,128)(2,1)}) %all-gather.3.cloned.1.call-update) | async-done | bytes 1572880 | tf_op jit(solution)/shard_map/while/body/eval_jaxpr/all_gather | solution.py:119
  68.2 29.0 %all-gather.5.cloned.1.call-done = bf16[2,512,768]{2,1,0:T(8,128)(2,1)} async-done(((bf16[2,128,768]{2,1,0:T(8,128)(2,1)}), bf16[2,512,768]{2,1,0:T(8,128)(2,1)}) %all-gather.5.cloned.1.call-update) | async-done | bytes 1572880 | tf_op jit(solution)/shard_map/while/body/eval_jaxpr/all_gather | solution.py:120
  116.7 5.6 multiply_reduce_fusion.9
  145.3 6.4 fusion.233
  153.6 6.5 fusion.232
  178.4 24.7 %reduce-scatter.23.cloned.1.call-done = bf16[2,128,768]{2,1,0:T(8,128)(2,1)} async-done(((bf16[2,512,768]{2,1,0:T(8,128)(2,1)}), bf16[2,128,768]{2,1,0:T(8,128)(2,1)}) %reduce-scatter.23.cloned.1.call-update) | async-done | bytes 393232 | tf_op jit(solution)/shard_map/while/body/eval_jaxpr/reduce_scatter | solution.py:195
  230.4 21.7 %all-gather.3.cloned.1.call-done = bf16[2,512,768]{2,1,0:T(8,128)(2,1)} async-done(((bf16[2,128,768]{2,1,0:T(8,128)(2,1)}), bf16[2,512,768]{2,1,0:T(8,128)(2,1)}) %all-gather.3.cloned.1.call-update) | async-done | bytes 1572880 | tf_op jit(solution)/shard_map/while/body/eval_jaxpr/all_gather | solution.py:119
  260.3 29.3 %all-gather.5.cloned.1.call-done = bf16[2,512,768]{2,1,0:T(8,128)(2,1)} async-done(((bf16[2,128,768]{2,1,0:T(8,128)(2,1)}), bf16[2,512,768]{2,1,0:T(8,128)(2,1)}) %all-gather.5.cloned.1.call-update) | async-done | bytes 1572880 | tf_op jit(solution)/shard_map/while/body/eval_jaxpr/all_gather | solution.py:120
  337.7 6.4 fusion.233
  346.0 6.5 fusion.232
  358.7 9.0 %select_add_fusion.20 = f32[768,3072]{1,0:T(8,128)} fusion(f32[768,3072]{1,0:T(8,128)} %get-tuple-element.736, bf16[256,3072]{1,0:T(8,128)(2,1)S(1)} %copy-done.36, pred[]{:T(512)S(6)} %compare.3, f32[256,768]{1,0:T(8,128)S(1)} %copy-done.8, f32[768]{0:T(1024)S(1)} %copy-done.43, f32[256]{0:T(256)S(1)} %copy-done.49), kind=kOutput, calls=%fused_computation.1.clone.1 | convolution fusion | flops 1213267968 | bytes 21237760 | tf_op jit(solution)/shard_map/while/body/eval_jaxpr/dot_general | solution.py:66
  367.7 7.7 select_add_fusion.21
  378.2 17.5 %reduce-scatter.23.cloned.1.call-done = bf16[2,128,768]{2,1,0:T(8,128)(2,1)} async-done(((bf16[2,512,768]{2,1,0:T(8,128)(2,1)}), bf16[2,128,768]{2,1,0:T(8,128)(2,1)}) %reduce-scatter.23.cloned.1.call-update) | async-done | bytes 393232 | tf_op jit(solution)/shard_map/while/body/eval_jaxpr/reduce_scatter | solution.py:195
  408.8 41.2 %reduce-scatter.9.cloned.1.call-done = f32[96,768]{1,0:T(8,128)} async-done(((f32[768,768]{1,0:T(8,128)}), f32[96,768]{1,0:T(8,128)}) %reduce-scatter.9.cloned.1.call-update) | async-done | bytes 294928 | tf_op jit(solution)/shard_map/reduce_scatter | solution.py:249
  451.6 44.3 %reduce-scatter.11.cloned.1.call-done = f32[96,768]{1,0:T(8,128)} async-done(((f32[768,768]{1,0:T(8,128)}), f32[96,768]{1,0:T(8,128)}) %reduce-scatter.11.cloned.1.call-update) | async-done | bytes 294928 | tf_op jit(solution)/shard_map/reduce_scatter | solution.py:249
  497.6 43.9 %reduce-scatter.13.cloned.1.call-done = f32[96,768]{1,0:T(8,128)} async-done(((f32[768,768]{1,0:T(8,128)}), f32[96,768]{1,0:T(8,128)}) %reduce-scatter.13.cloned.1.call-update) | async-done | bytes 294928 | tf_op jit(solution)/shard_map/reduce_scatter | solution.py:249
  543.1 44.5 %reduce-scatter.15.cloned.1.call-done = f32[96,768]{1,0:T(8,128)} async-done(((f32[768,768]{1,0:T(8,128)}), f32[96,768]{1,0:T(8,128)}) %reduce-scatter.15.cloned.1.call-update) | async-done | bytes 294928 | tf_op jit(solution)/shard_map/reduce_scatter | solution.py:249
  589.3 78.2 %reduce-scatter.17.cloned.1.call-done = f32[96,3072]{1,0:T(8,128)} async-done(((f32[768,3072]{1,0:T(8,128)}), f32[96,3072]{1,0:T(8,128)}) %reduce-scatter.17.cloned.1.call-update) | async-done | bytes 1179664 | tf_op jit(solution)/shard_map/reduce_scatter | solution.py:249
  669.6 77.7 %reduce-scatter.19.cloned.1.call-done = f32[384,768]{1,0:T(8,128)} async-done(((f32[3072,768]{1,0:T(8,128)}), f32[384,768]{1,0:T(8,128)}) %reduce-scatter.19.cloned.1.call-update) | async-done | bytes 1179664 | tf_op jit(solution)/shard_map/reduce_scatter | solution.py:249
  750.7 13.4 %all-reduce.2 = (bf16[768]{0:T(1024)(128)(2,1)S(1)}, bf16[768]{0:T(1024)(128)(2,1)S(1)}) all-reduce(f32[768]{0:T(1024)S(1)} %copy-done.61, f32[768]{0:T(1024)S(1)} %copy-done.64), channel_id=10, replica_groups=mesh['dp'=8,'seq'=4] {'dp'}, use_global_device_ids=true, to_apply=%region_26.27.clone | all-reduce | flops 1536 | bytes 9216
  764.3 12.4 %all-reduce.3 = (bf16[96]{0:T(256)(128)(2,1)S(1)}, bf16[96]{0:T(256)(128)(2,1)S(1)}) all-reduce(bf16[96]{0:T(256)(128)(2,1)S(1)} %dynamic-slice.7, bf16[96]{0:T(256)(128)(2,1)S(1)} %dynamic-slice.6), channel_id=1, replica_groups=mesh['dp'=8,'seq'=4] {'seq'}, use_global_device_ids=true, to_apply=%region_27.28 | all-reduce | flops 192 | bytes 768 | tf_op jit(solution)/shard_map/psum | solution.py:250
  777.7 38.2 %psum.71 = f32[32,12]{0,1:T(8,128)} all-reduce(f32[32,12]{0,1:T(8,128)S(1)} %copy-done.54), channel_id=1, replica_groups=mesh['dp'=8,'seq'=4] {'dp','seq'}, use_global_device_ids=true, to_apply=%region_30.31 | all-reduce | flops 384 | bytes 3072 | tf_op jit(solution)/shard_map/psum | solution.py:251
  816.0 12.7 %all-reduce.7.cloned.1.call-done = (bf16[96,768]{1,0:T(8,128)(2,1)}, bf16[96,768]{1,0:T(8,128)(2,1)}, bf16[96,768]{1,0:T(8,128)(2,1)}, bf16[96,768]{1,0:T(8,128)...) async-done(((bf16[96,768]{1,0:T(8,128)(2,1)}, bf16[96,768]{1,0:T(8,128)(2,1)}, bf16[96,768]{1,0:T(8,128)(2,1)}, bf16[96,768]{1,0:T(8,128)(2,1)}, ...) | async-done | bytes 1769488 | tf_op jit(solution)/shard_map/psum | solution.py:250
  (466 shorter events, 220.2 us)
Async XLA Ops:
  14.0 45.6 %all-gather.3.cloned.1.call-start = ((), (), s32[]{:S(2)}) async-start(), calls=%async_computation.15 | async-start | bytes 1966080 | tf_op jit(solution)/shard_map/while/body/eval_jaxpr/all_gather | solution.py:119
  19.7 77.6 %all-gather.5.cloned.1.call-start = ((), (), s32[]{:S(2)}) async-start(), calls=%async_computation.16 | async-start | bytes 1966080 | tf_op jit(solution)/shard_map/while/body/eval_jaxpr/all_gather | solution.py:120
  21.0 154.7 %reduce-scatter.21.cloned.1.call-start = ((), (), s32[]{:S(2)}) async-start(), calls=%async_computation.17 | async-start | bytes 1966080 | tf_op jit(solution)/shard_map/while/body/eval_jaxpr/reduce_scatter | solution.py:192
  68.2 30.8 %copy-start.41 = (f32[2,12,128]{2,1,0:T(8,128)S(1)}, f32[2,12,128]{2,1,0:T(8,128)}, u32[]{:S(2)}) copy-start(f32[2,12,128]{2,1,0:T(8,128)} %copy-done.40) | copy-start | bytes 36868 | tf_op jit(solution)/shard_map/while
  132.3 70.9 %reduce-scatter.23.cloned.1.call-start = ((), (), s32[]{:S(2)}) async-start(), calls=%async_computation.18 | async-start | bytes 1966080 | tf_op jit(solution)/shard_map/while/body/eval_jaxpr/reduce_scatter | solution.py:195
  175.7 27.5 %copy-start.47 = (f32[256]{0:T(256)S(1)}, f32[256]{0:T(256)}, u32[]{:S(2)}) copy-start(f32[256]{0:T(256)} %copy-done.46) | copy-start | bytes 3076 | tf_op jit(solution)/shard_map/while
  175.7 29.9 %copy-start.51 = (f32[2,128]{1,0:T(2,128)S(1)}, f32[2,128]{1,0:T(2,128)}, u32[]{:S(2)}) copy-start(f32[2,128]{1,0:T(2,128)} %copy-done.50) | copy-start | bytes 3076 | tf_op jit(solution)/shard_map/while
  175.7 29.9 %copy-start.13 = (bf16[1,2,128,768]{3,2,1,0:T(8,128)(2,1)S(1)}, bf16[1,2,128,768]{3,2,1,0:T(8,128)(2,1)}, u32[]{:S(2)}) copy-start(bf16[1,2,128,768]{3,2,1,0:T(8,128)(2,1)} %fusion.216) | copy-start | bytes 1179652 | tf_op jit(solution)/shard_map/while
  210.2 41.9 %all-gather.3.cloned.1.call-start = ((), (), s32[]{:S(2)}) async-start(), calls=%async_computation.15 | async-start | bytes 1966080 | tf_op jit(solution)/shard_map/while/body/eval_jaxpr/all_gather | solution.py:119
  215.9 73.7 %all-gather.5.cloned.1.call-start = ((), (), s32[]{:S(2)}) async-start(), calls=%async_computation.16 | async-start | bytes 1966080 | tf_op jit(solution)/shard_map/while/body/eval_jaxpr/all_gather | solution.py:120
  217.2 158.2 %reduce-scatter.21.cloned.1.call-start = ((), (), s32[]{:S(2)}) async-start(), calls=%async_computation.17 | async-start | bytes 1966080 | tf_op jit(solution)/shard_map/while/body/eval_jaxpr/reduce_scatter | solution.py:192
  260.3 31.1 %copy-start.41 = (f32[2,12,128]{2,1,0:T(8,128)S(1)}, f32[2,12,128]{2,1,0:T(8,128)}, u32[]{:S(2)}) copy-start(f32[2,12,128]{2,1,0:T(8,128)} %copy-done.40) | copy-start | bytes 36868 | tf_op jit(solution)/shard_map/while
  324.7 71.0 %reduce-scatter.23.cloned.1.call-start = ((), (), s32[]{:S(2)}) async-start(), calls=%async_computation.18 | async-start | bytes 1966080 | tf_op jit(solution)/shard_map/while/body/eval_jaxpr/reduce_scatter | solution.py:195
  404.7 45.2 %reduce-scatter.9.cloned.1.call-start = ((), (), s32[]{:S(2)}) async-start(), calls=%async_computation.8 | async-start | bytes 2654208 | tf_op jit(solution)/shard_map/reduce_scatter | solution.py:249
  405.3 90.6 %reduce-scatter.11.cloned.1.call-start = ((), (), s32[]{:S(2)}) async-start(), calls=%async_computation.9 | async-start | bytes 2654208 | tf_op jit(solution)/shard_map/reduce_scatter | solution.py:249
  405.9 135.6 %reduce-scatter.13.cloned.1.call-start = ((), (), s32[]{:S(2)}) async-start(), calls=%async_computation.10 | async-start | bytes 2654208 | tf_op jit(solution)/shard_map/reduce_scatter | solution.py:249
  406.5 181.1 %reduce-scatter.15.cloned.1.call-start = ((), (), s32[]{:S(2)}) async-start(), calls=%async_computation.11 | async-start | bytes 2654208 | tf_op jit(solution)/shard_map/reduce_scatter | solution.py:249
  407.2 260.2 %reduce-scatter.17.cloned.1.call-start = ((), (), s32[]{:S(2)}) async-start(), calls=%async_computation.12 | async-start | bytes 10616832 | tf_op jit(solution)/shard_map/reduce_scatter | solution.py:249
  408.0 339.3 %reduce-scatter.19.cloned.1.call-start = ((), (), s32[]{:S(2)}) async-start(), calls=%async_computation.13 | async-start | bytes 10616832 | tf_op jit(solution)/shard_map/reduce_scatter | solution.py:249
  408.7 420.0 %all-reduce.7.cloned.1.call-start = ((), (), s32[]{:S(2)}) async-start(), calls=%async_computation.14 | async-start | bytes 3538944 | tf_op jit(solution)/shard_map/psum | solution.py:250
  497.6 251.9 %copy-start.68 = (u32[32]{0:T(128)S(1)}, u32[32]{0:T(128)}, u32[]{:S(2)}) copy-start(u32[32]{0:T(128)} %constant.154) | copy-start | bytes 388
  497.6 253.2 %copy-start.61 = (f32[768]{0:T(1024)S(1)}, f32[768]{0:T(1024)}, u32[]{:S(2)}) copy-start(f32[768]{0:T(1024)} %get-tuple-element.346) | copy-start | bytes 9220
  497.6 253.2 %copy-start.64 = (f32[768]{0:T(1024)S(1)}, f32[768]{0:T(1024)}, u32[]{:S(2)}) copy-start(f32[768]{0:T(1024)} %get-tuple-element.347) | copy-start | bytes 9220
  497.6 280.2 %copy-start.54 = (f32[32,12]{0,1:T(8,128)S(1)}, f32[32,12]{0,1:T(8,128)}, u32[]{:S(2)}) copy-start(f32[32,12]{0,1:T(8,128)} %get-tuple-element.348) | copy-start | bytes 4612
  (133 other events, 651.1 us)
Sparse Core Ops, SparseCore 0:
  19.8 39.7 all-gather.2
  61.3 35.9 all-gather.4
  132.4 34.1 reduce-scatter.20
  168.8 34.2 reduce-scatter.22
  216.0 36.0 all-gather.2
  253.6 35.9 all-gather.4
  324.8 34.1 reduce-scatter.20
  361.4 34.2 reduce-scatter.22
Sparse Core Ops, SparseCore 1:
  408.6 41.3 reduce-scatter.8
  453.5 42.3 reduce-scatter.10
  499.1 42.3 reduce-scatter.12
  545.2 42.3 reduce-scatter.14
  591.1 76.3 reduce-scatter.16
  671.0 76.3 reduce-scatter.18
  750.6 78.0 all-reduce.6
where the time goes:
time: 846 us; the launch traced here: 844 us
  waiting for transfers between devices  494 us (58%)
  matrix products  158 us (19%)
  blocking collectives  64 us (8%)
  local copies, waits for them, and re-layouts  57.7 us (7%)
  other arithmetic  47.9 us (6%)
  between operations  16.6 us (2%)
    reduce_scatter x6, waiting for transfers between devices, on_device(): lax.psum_scatter(local_grads, 'dp', scatter_dimension=0, tiled=True)  330 us
    all_gather x2, waiting for transfers between devices, micro_step(): lax.all_gather(value_three, 'seq', axis=1, tiled=True)  58.4 us
    all_gather x2, waiting for transfers between devices, micro_step(): lax.all_gather(key_three, 'seq', axis=1, tiled=True)  47.1 us
    reduce_scatter x2, waiting for transfers between devices, micro_step(): lax.psum_scatter(value_terms.astype(jnp.bfloat16), 'seq', scatter_dimensi...  42.2 us
    psum x1, blocking collectives, on_device(): table_total = lax.psum(totals[8], ('dp', 'seq'))  38.2 us
    dot_general x12, matrix products, outer_sum(): lax.dot_general(left, right, (((0,), (0,)), ((), ())), preferred_element_...  38 us
    dot_general x12, matrix products, back_dot(): lax.dot_general(grad_rows, weight, (((1,), (1,)), ((), ())), preferred_el...  24.7 us
    while x268, local copies, waits for them, and re-layouts  20.4 us
  transfers between devices with their start and end apart: 15, of which 13 were waited for; matrix products, arithmetic and copies ran while one was open for 17% of the time, Pallas kernels for 0%

commit v1 on v0

v1 whole, which is shorter than its diff:
```python
from functools import partial

import jax
import jax.numpy as jnp
from jax import lax
from jax.sharding import PartitionSpec as P

EPS = 1e-06
NEG = -1000000000.0
LIMITS = (12, 16, 23, 32, 46, 64, 91)
HIGH = lax.Precision.HIGHEST


def rms_scale(values, gain_vec):
    factor = lax.rsqrt(jnp.mean(values * values, axis=-1, keepdims=True) + EPS)
    return values * factor * gain_vec


def buckets(relative):
    distance = jnp.abs(relative)
    far_bucket = 8 + sum(((distance >= thresh).astype(jnp.int32) for thresh in LIMITS))
    return jnp.where(relative > 0, 16, 0) + jnp.where(distance < 8, distance, far_bucket)


def position_bias(table_f, query_pos, key_pos):
    relative = key_pos[None, :] - query_pos[:, None]
    bucket_count, head_count = table_f.shape
    one_hot = (buckets(relative)[:, :, None] == jnp.arange(bucket_count)[None, None, :]).astype(
        jnp.float32
    )
    one_hot = one_hot.reshape(query_pos.shape[0] * key_pos.shape[0], bucket_count)
    pos_bias = jnp.dot(one_hot, table_f, precision=HIGH).reshape(
        query_pos.shape[0], key_pos.shape[0], head_count
    )
    return (one_hot, pos_bias.transpose(2, 0, 1))


def split_heads(arr, head_count):
    return arr.reshape(arr.shape[0], arr.shape[1], head_count, arr.shape[2] // head_count)


def scores_of(query_rows, key_rows, pos_bias, key_live):
    head_count = pos_bias.shape[0]
    scores = jnp.einsum(
        "rqhd,rkhd->rhqk",
        split_heads(query_rows, head_count),
        split_heads(key_rows, head_count),
        preferred_element_type=jnp.float32,
    )
    scores = scores + pos_bias[None]
    return jnp.where(key_live[:, None, None, :], scores, NEG)


def outer_sum(left, right):
    return lax.dot_general(
        left, right, (((0,), (0,)), ((), ())), preferred_element_type=jnp.float32
    )


def back_dot(grad_rows, weight):
    return lax.dot_general(
        grad_rows, weight, (((1,), (1,)), ((), ())), preferred_element_type=jnp.float32
    )


def on_device(
    hidden_in,
    query_lengths,
    doc_lengths,
    w_query,
    w_key,
    w_value,
    w_attn_out,
    w_inner,
    w_outer,
    gain_attn,
    gain_ffn,
    bias_table,
    cotangent,
):
    def to_rows(blocks):
        return lax.all_to_all(blocks, "seq", split_axis=0, concat_axis=1, tiled=True)

    def to_blocks(rows):
        return lax.all_to_all(rows, "seq", split_axis=1, concat_axis=0, tiled=True)

    hidden_rows = to_rows(hidden_in)
    cot_rows = to_rows(cotangent)
    row_count, length, width = hidden_rows.shape
    head_count = bias_table.shape[1]
    tokens = row_count * length
    first = lax.axis_index("seq") * row_count
    total_len = lax.dynamic_slice_in_dim(query_lengths + doc_lengths, first, row_count)
    gain_one = gain_attn.astype(jnp.float32)
    gain_two = gain_ffn.astype(jnp.float32)
    table_f = bias_table.astype(jnp.float32)

    def low_dot(rows, weight):
        return jnp.dot(rows, weight, preferred_element_type=jnp.float32).astype(jnp.bfloat16)

    resid_in = hidden_rows.astype(jnp.float32).reshape(tokens, width)
    cot_flat = cot_rows.reshape(tokens, width)
    normed_one = rms_scale(resid_in, gain_one).astype(jnp.bfloat16)
    query_low = low_dot(normed_one, w_query).reshape(row_count, length, width)
    key_low = low_dot(normed_one, w_key).reshape(row_count, length, width)
    value_low = low_dot(normed_one, w_value).reshape(row_count, length, width)
    pos = jnp.arange(length)
    key_live = pos[None, :] < total_len[:, None]
    one_hot, pos_bias = position_bias(table_f, pos, pos)
    scores = scores_of(query_low, key_low, pos_bias, key_live)
    row_max = jnp.max(scores, axis=-1, keepdims=True)
    exponent = jnp.exp(scores - row_max)
    probs = exponent / jnp.sum(exponent, axis=-1, keepdims=True)
    probs_low = probs.astype(jnp.bfloat16)
    value_heads = split_heads(value_low, head_count)
    attended_low = (
        jnp.einsum("rhqk,rkhd->rqhd", probs_low, value_heads, preferred_element_type=jnp.float32)
        .reshape(tokens, width)
        .astype(jnp.bfloat16)
    )
    resid_mid = resid_in + jnp.dot(attended_low, w_attn_out, preferred_element_type=jnp.float32)
    normed_two = rms_scale(resid_mid, gain_two).astype(jnp.bfloat16)
    inner = jnp.dot(normed_two, w_inner, preferred_element_type=jnp.float32)
    gelu_out, gelu_back = jax.vjp(partial(jax.nn.gelu, approximate=True), inner)
    active = gelu_out.astype(jnp.bfloat16)
    layer_rows = (
        (resid_mid + jnp.dot(active, w_outer, preferred_element_type=jnp.float32))
        .astype(jnp.bfloat16)
        .reshape(row_count, length, width)
    )
    grad_outer_w = outer_sum(active, cot_flat).astype(jnp.bfloat16)
    grad_inner_low = gelu_back(back_dot(cot_flat, w_outer))[0].astype(jnp.bfloat16)
    grad_inner_w = outer_sum(normed_two, grad_inner_low).astype(jnp.bfloat16)
    grad_normed_two = back_dot(grad_inner_low, w_inner)
    norm_out, norm_two_back = jax.vjp(rms_scale, resid_mid, gain_two)
    grad_mid_norm, gain_two_grad = norm_two_back(grad_normed_two)
    grad_mid = cot_flat.astype(jnp.float32) + grad_mid_norm
    grad_mid_low = grad_mid.astype(jnp.bfloat16)
    grad_attn_out_w = outer_sum(attended_low, grad_mid_low).astype(jnp.bfloat16)
    grad_attended = back_dot(grad_mid_low, w_attn_out).astype(jnp.bfloat16)
    grad_heads = split_heads(grad_attended.reshape(row_count, length, width), head_count)
    grad_prob = jnp.einsum(
        "rqhd,rkhd->rhqk", grad_heads, value_heads, preferred_element_type=jnp.float32
    )
    delta = jnp.sum(probs * grad_prob, axis=-1, keepdims=True)
    dscore = (probs * (grad_prob - delta)).astype(jnp.bfloat16)
    key_heads = split_heads(key_low, head_count)
    query_heads = split_heads(query_low, head_count)

    def joined(heads):
        return heads.reshape(tokens, width).astype(jnp.bfloat16)

    grad_query_low = joined(
        jnp.einsum("rhqk,rkhd->rqhd", dscore, key_heads, preferred_element_type=jnp.float32)
    )
    grad_key_low = joined(
        jnp.einsum("rhqk,rqhd->rkhd", dscore, query_heads, preferred_element_type=jnp.float32)
    )
    grad_value_low = joined(
        jnp.einsum("rhqk,rqhd->rkhd", probs_low, grad_heads, preferred_element_type=jnp.float32)
    )
    score_sum = jnp.sum(dscore, axis=0, dtype=jnp.float32).reshape(head_count, length * length)
    table_grad = lax.dot_general(one_hot, score_sum, (((0,), (1,)), ((), ())), precision=HIGH)
    grad_query_w = outer_sum(normed_one, grad_query_low).astype(jnp.bfloat16)
    grad_key_w = outer_sum(normed_one, grad_key_low).astype(jnp.bfloat16)
    grad_value_w = outer_sum(normed_one, grad_value_low).astype(jnp.bfloat16)
    grad_normed_one = (
        back_dot(grad_query_low, w_query)
        + back_dot(grad_key_low, w_key)
        + back_dot(grad_value_low, w_value)
    )
    norm_first, norm_one_back = jax.vjp(rms_scale, resid_in, gain_one)
    grad_resid_norm, gain_one_grad = norm_one_back(grad_normed_one)
    grad_rows = (grad_mid + grad_resid_norm).astype(jnp.bfloat16)
    layer_out = to_blocks(layer_rows)
    grad_in = to_blocks(grad_rows.reshape(row_count, length, width))

    def share(part):
        piece = lax.psum_scatter(part, "dp", scatter_dimension=0, tiled=True)
        return lax.psum(piece, "seq").astype(jnp.float32)

    small = jnp.concatenate([gain_one_grad, gain_two_grad, table_grad.reshape(-1)])
    small = lax.psum(small, ("dp", "seq"))
    gain_rows = width // lax.axis_size("dp")
    gain_at = lax.axis_index("dp") * gain_rows
    return (
        layer_out,
        grad_in,
        share(grad_query_w),
        share(grad_key_w),
        share(grad_value_w),
        share(grad_attn_out_w),
        share(grad_inner_w),
        share(grad_outer_w),
        lax.dynamic_slice_in_dim(small, gain_at, gain_rows),
        lax.dynamic_slice_in_dim(small, width + gain_at, gain_rows),
        small[2 * width :].reshape(bias_table.shape),
    )


def solution(mesh):
    return jax.shard_map(
        on_device,
        mesh=mesh,
        in_specs=(
            P("dp", "seq", None),
            P("dp"),
            P("dp"),
            P(),
            P(),
            P(),
            P(),
            P(),
            P(),
            P(),
            P(),
            P(),
            P("dp", "seq", None),
        ),
        out_specs=(
            P("dp", "seq", None),
            P("dp", "seq", None),
            P("dp", None),
            P("dp", None),
            P("dp", None),
            P("dp", None),
            P("dp", None),
            P("dp", None),
            P("dp"),
            P("dp"),
            P(),
        ),
        check_vma=False,
    )
```

time: 846 us -> 522 us (0.62)
  waiting for transfers between devices: 494 us -> 162 us
  blocking collectives: 64 us -> 41.1 us
  starting transfers between devices: 0.64 us -> 22.6 us
  matrix products: 158 us -> 141 us
  local copies, waits for them, and re-layouts: 57.7 us -> 74.5 us
  other arithmetic: 47.9 us -> 60.7 us
    reduce_scatter x10 -> x6, waiting for transfers between devices: 372 us -> 158 us  [share(): piece = lax.psum_scatter(part, 'dp', scatter_dimension=0, tiled=True)]
    all_gather x4 -> x0, waiting for transfers between devices: 105 us -> none  [the longest x2 58.4 us: micro_step(): lax.all_gather(value_three, 'seq', axis=1, tiled=True)]
    unnamed x19 -> x70, local copies, waits for them, and re-layouts: 0.77 us -> 37.7 us
    all_to_all x0 -> x4, starting transfers between devices: none -> 21.6 us  [the longest x2 11.6 us: to_rows(): lax.all_to_all(blocks, 'seq', split_axis=0, concat_axis=1, tiled=True)]
    while x268 -> x0, local copies, waits for them, and re-layouts: 20.4 us -> none
    dot_general x0 -> x1, local copies, waits for them, and re-layouts: none -> 17.9 us  [position_bias(): jnp.dot(one_hot, table_f, precision=HIGH)]
    sub x0 -> x1, other arithmetic: none -> 15.8 us  [on_device(): exponent = jnp.exp(scores - row_max)]
    unnamed x9 -> x5, other arithmetic: 0.01 us -> 14 us
  transfers between devices with their start and end apart: 15 -> 11, of which waited for: 13 -> 5; matrix products, arithmetic and copies ran while one was open for 17% -> 46% of each run, Pallas kernels for 0% -> 0%
where the time goes in v1:
time: 522 us; the launch traced here: 517 us
  waiting for transfers between devices  162 us (31%)
  matrix products  141 us (27%)
  local copies, waits for them, and re-layouts  74.5 us (14%)
  other arithmetic  60.7 us (12%)
  blocking collectives  41.1 us (8%)
  starting transfers between devices  22.6 us (4%)
  between operations  14.8 us (3%)
    reduce_scatter x6, waiting for transfers between devices, share(): piece = lax.psum_scatter(part, 'dp', scatter_dimension=0, tiled=True)  158 us
    psum x1, blocking collectives, on_device(): small = lax.psum(small, ('dp', 'seq'))  41.1 us
    unnamed x70, local copies, waits for them, and re-layouts  37.7 us
    dot_general x6, matrix products, outer_sum(): lax.dot_general(left, right, (((0,), (0,)), ((), ())), preferred_element_...  24.4 us
    dot_general x1, local copies, waits for them, and re-layouts, position_bias(): jnp.dot(one_hot, table_f, precision=HIGH)  17.9 us
    dot_general x6, matrix products, back_dot(): lax.dot_general(grad_rows, weight, (((1,), (1,)), ((), ())), preferred_el...  17.2 us
    sub x1, other arithmetic, on_device(): exponent = jnp.exp(scores - row_max)  15.8 us
    unnamed x5, other arithmetic  14 us
  transfers between devices with their start and end apart: 11, of which 5 were waited for; matrix products, arithmetic and copies ran while one was open for 46% of the time, Pallas kernels for 0%

profile of v1, /device:TPU:0, one launch (start us, length us, event | category | flops | bytes accessed | tf_op | source)
XLA Modules:
  0.0 516.8 jit_solution(13536951761732378197)
XLA Ops:
  7.2 6.5 %all-to-all-start = ((bf16[4,128,768]{2,1,0:T(8,128)(2,1)}), bf16[4,128,768]{2,1,0:T(8,128)(2,1)S(1)}, u32[]{:S(2)}, u32[]{:S(2)}) async-start(bf16[4,128,768]{2,1,0:T(8,128)(2,1)} %param.13), calls=%async_computation | async-start | bytes 1572864 | tf_op jit(solution)/shard_map/all_to_all | solution.py:82
  15.4 9.2 %fusion.1 = f32[512,512,12]{1,2,0:T(8,128)} fusion(s32[512,512]{1,0:T(8,128)S(1)} %select_add_fusion, bf16[32,12]{0,1:T(8,128)(2,1)} %param.24), kind=kOutput, calls=%fused_computation.3 | convolution fusion | flops 209715200 | bytes 13632256 | tf_op jit(solution)/shard_map/dot_general | solution.py:32
  24.6 17.9 %copy.80 = f32[512,512,12]{0,1,2:T(8,128)} copy(f32[512,512,12]{1,2,0:T(8,128)} %fusion.1) | data formatting | bytes 25165824 | tf_op jit(solution)/shard_map/dot_general | solution.py:32
  59.4 12.1 %fusion.5 = f32[12,512,512]{1,2,0:T(8,128)} fusion(f32[512,512,12]{0,1,2:T(8,128)} %copy.80, pred[512]{0:T(512)(128)(4,1)} %iota_compare_fusion.4, bf16[512,12,64]{0,2,1:T(8,128)(2,1)S(1)} %bitcast.129, bf16[512,12,64]{0,2,1:T(8,128)(2,1)S(1)} %bitcast.126), kind=kOutput, calls=%fused_computation.8 | convolution fusion | flops 408944640 | bytes 26739200 | tf_op jit(solution)/shard_map/rqhd,rkhd->rhqk/dot_general | solution.py:44
  71.4 15.8 %fusion.53 = (f32[12,512]{1,0:T(8,128)}, f32[12,512,512]{1,2,0:T(8,128)}) fusion(f32[12,512,512]{1,2,0:T(8,128)} %fusion.5), kind=kOutput, calls=%fused_computation.98 | output fusion | flops 6291967 | bytes 25190400 | tf_op jit(solution)/shard_map/sub | solution.py:112
  89.0 12.1 %fusion.28 = bf16[12,64,512]{2,1,0:T(8,128)(2,1)} fusion(bf16[512,12,64]{0,2,1:T(8,128)(2,1)S(1)} %bitcast.142, f32[12,512]{1,0:T(8,128)} %get-tuple-element.67, f32[12,512,512]{1,2,0:T(8,128)} %fusion.5), kind=kOutput, calls=%fused_computation.64 | convolution fusion | flops 412490240 | bytes 14180352 | tf_op jit(solution)/shard_map/rhqk,rkhd->rqhd/dot_general | solution.py:117
  110.0 9.6 %fusion.12 = (bf16[512,3072]{1,0:T(8,128)(2,1)S(1)}, f32[512,3072]{1,0:T(8,128)}) fusion(f32[512,3072]{1,0:T(8,128)S(1)} %fusion.54, bf16[768,3072]{1,0:T(8,128)(2,1)} %param.20, f32[512,768]{1,0:T(8,128)S(1)} %get-tuple-element.70, f32[768]{0:T(1024)S(1)} %convert_element_type.260, f32[512]{0:T(512)S(1)} %copy-done.20), kind=kOutput, calls=%fused_computation.20 | convolution fusion | flops 2448556032 | bytes 22025216 | tf_op jit(solution)/shard_map/dot_general | solution.py:123
  132.4 12.7 %fusion.31 = bf16[12,64,512]{2,1,0:T(8,128)(2,1)} fusion(bf16[512,12,64]{0,2,1:T(8,128)(2,1)} %bitcast.147, f32[12,512]{1,0:T(8,128)} %get-tuple-element.67, f32[12,512,512]{1,2,0:T(8,128)} %fusion.5), kind=kOutput, calls=%fused_computation.65 | convolution fusion | flops 412490240 | bytes 14180352 | tf_op jit(solution)/shard_map/rhqk,rqhd->rkhd/dot_general | solution.py:160
  150.0 12.2 %multiply_reduce_fusion = (f32[12,512]{1,0:T(8,128)}, f32[12,512,512]{1,2,0:T(8,128)}) fusion(f32[12,512,512]{1,2,0:T(8,128)} %get-tuple-element.68, f32[12,512]{1,0:T(8,128)} %get-tuple-element.67, bf16[512,12,64]{0,2,1:T(8,128)(2,1)} %bitcast.148, bf16[512,12,64]{0,2,1:T(8,128)(2,1)} %bitcast.143), kind=kOutput, calls=%fused_computation.10 | convolution fusion | flops 412084224 | bytes 26787840 | tf_op jit(solution)/shard_map/rqhd,rkhd->rhqk/dot_general | solution.py:142
  162.3 9.9 %multiply_convert_fusion = bf16[12,512,512]{1,2,0:T(8,128)(2,1)S(1)} fusion(f32[12,512,512]{1,2,0:T(8,128)} %get-tuple-element.75, f32[12,512]{1,0:T(8,128)} %get-tuple-element.74, f32[12,512,512]{1,2,0:T(8,128)} %get-tuple-element.68, f32[12,512]{1,0:T(8,128)} %get-tuple-element.67), kind=kLoop, calls=%fused_computation.9 | loop fusion | flops 12582912 | bytes 31506432 | tf_op jit(solution)/shard_map/convert_element_type | solution.py:146
  177.8 5.3 %convolution_convert_fusion.10 = bf16[12,64,512]{2,1,0:T(8,128)(2,1)S(1)} fusion(bf16[512,12,64]{0,2,1:T(8,128)(2,1)} %bitcast.130, bf16[12,512,512]{1,2,0:T(8,128)(2,1)} %copy-done.1), kind=kOutput, calls=%fused_computation.66 | convolution fusion | flops 403046400 | bytes 7864320 | tf_op jit(solution)/shard_map/rhqk,rqhd->rkhd/dot_general | solution.py:157
  185.9 8.5 %convolution_convert_fusion = bf16[3072,768]{1,0:T(8,128)(2,1)} fusion(bf16[512,768]{1,0:T(8,128)(2,1)} %bitcast.12, f32[512,3072]{1,0:T(8,128)} %get-tuple-element.72), kind=kOutput, calls=%fused_computation.23 | convolution fusion | flops 2432434176 | bytes 11796480 | tf_op jit(solution)/shard_map/dot_general | solution.py:55
  194.9 7.3 %convolution_convert_fusion.1 = bf16[768,3072]{1,0:T(8,128)(2,1)} fusion(bf16[512,3072]{1,0:T(8,128)(2,1)} %copy-done.26, f32[512,768]{1,0:T(8,128)} %copy-done.8, f32[768]{0:T(1024)S(1)} %convert_element_type.260, f32[512]{0:T(512)} %fusion.49), kind=kOutput, calls=%fused_computation.24 | convolution fusion | flops 2419458048 | bytes 9442304 | tf_op jit(solution)/shard_map/dot_general | solution.py:55
  205.0 8.0 %fusion.34 = bf16[1,512,768]{2,1,0:T(8,128)(2,1)S(1)} fusion(f32[512,768]{1,0:T(8,128)S(1)} %copy-done.9, bf16[3072,768]{1,0:T(8,128)(2,1)} %param.21, f32[512,3072]{1,0:T(8,128)} %get-tuple-element.72), kind=kOutput, calls=%fused_computation.70 | convolution fusion | flops 2430861312 | bytes 13369344 | tf_op jit(solution)/shard_map/dot_general | solution.py:127
  215.8 7.5 %reduce.10 = bf16[512,768]{1,0:T(8,128)(2,1)} reduce(bf16[512,1,768]{2,1,0:T(2,128)(2,1)} %bitcast.131, bf16[]{:T(256)} %broadcast.260), dimensions={1}, to_apply=%bitcast.124.reduce_sub_computation | reduce | bytes 1572866
  238.3 6.3 %reduce.11 = bf16[512,768]{1,0:T(8,128)(2,1)} reduce(bf16[512,1,768]{2,1,0:T(2,128)(2,1)S(1)} %bitcast.132, bf16[]{:T(256)} %broadcast.260), dimensions={1}, to_apply=%bitcast.123.reduce_sub_computation | reduce | bytes 1572866
  249.3 40.8 %reduce-scatter.9.cloned.1.call-done = bf16[96,768]{1,0:T(8,128)(2,1)} async-done(((bf16[768,768]{1,0:T(8,128)(2,1)}), bf16[96,768]{1,0:T(8,128)(2,1)}) %reduce-scatter.9.cloned.1.call-update) | async-done | bytes 147472 | tf_op jit(solution)/shard_map/reduce_scatter | solution.py:179
  290.1 57.2 %reduce-scatter.17.cloned.1.call-done = bf16[384,768]{1,0:T(8,128)(2,1)} async-done(((bf16[3072,768]{1,0:T(8,128)(2,1)}), bf16[384,768]{1,0:T(8,128)(2,1)}) %reduce-scatter.17.cloned.1.call-update) | async-done | bytes 589840 | tf_op jit(solution)/shard_map/reduce_scatter | solution.py:179
  347.3 57.6 %reduce-scatter.15.cloned.1.call-done = bf16[96,3072]{1,0:T(8,128)(2,1)} async-done(((bf16[768,3072]{1,0:T(8,128)(2,1)}), bf16[96,3072]{1,0:T(8,128)(2,1)}) %reduce-scatter.15.cloned.1.call-update) | async-done | bytes 589840 | tf_op jit(solution)/shard_map/reduce_scatter | solution.py:179
  411.6 8.7 %copy.88 = bf16[12,512,512]{2,1,0:T(8,128)(2,1)} copy(bf16[12,512,512]{1,2,0:T(8,128)(2,1)} %copy-done.1) | data formatting | bytes 12582912 | tf_op jit(solution)/shard_map/convert_element_type | solution.py:146
  420.3 6.7 %pad.3 = bf16[16,512,512]{2,1,0:T(8,128)(2,1)} pad(bf16[12,512,512]{2,1,0:T(8,128)(2,1)} %copy.88, bf16[]{:T(256)} %constant.72), padding=0_4x0_0x0_0 | pad | bytes 14680066
  427.0 11.5 %copy.100 = bf16[2,8,512,512]{3,1,2,0:T(8,128)(2,1)} copy(bf16[2,8,512,512]{3,2,1,0:T(8,128)(2,1)} %bitcast.125) | data formatting | bytes 16777216
  438.5 7.2 %fusion.2 = f32[32,12]{1,0:T(8,128)S(1)} fusion(bf16[12,262144]{1,0:T(8,128)(2,1)} %bitcast.128, s32[262144]{0:T(1024)S(1)} %copy-done.10), kind=kOutput, calls=%fused_computation.4 | convolution fusion | flops 209715200 | bytes 7341568 | tf_op jit(solution)/shard_map/dot_general | solution.py:163
  445.8 41.1 %psum.55 = f32[1920]{0:T(1024)S(1)} all-reduce(f32[1920]{0:T(1024)S(1)} %pad_maximum_fusion), channel_id=1, replica_groups=mesh['dp'=8,'seq'=4] {'dp','seq'}, use_global_device_ids=true, to_apply=%region_21.22 | all-reduce | flops 1920 | bytes 15360 | tf_op jit(solution)/shard_map/psum | solution.py:183
  (145 shorter events, 110.4 us)
Async XLA Ops:
  7.2 80.0 %copy-start = (bf16[768,768]{1,0:T(8,128)(2,1)S(1)}, bf16[768,768]{1,0:T(8,128)(2,1)}, u32[]{:S(2)}) copy-start(bf16[768,768]{1,0:T(8,128)(2,1)} %param.18) | copy-start | bytes 3538948
  7.2 37.1 %all-to-all-start = ((bf16[4,128,768]{2,1,0:T(8,128)(2,1)}), bf16[4,128,768]{2,1,0:T(8,128)(2,1)S(1)}, u32[]{:S(2)}, u32[]{:S(2)}) async-start(bf16[4,128,768]{2,1,0:T(8,128)(2,1)} %param.13), calls=%async_computation | async-start | bytes 1572864 | tf_op jit(solution)/shard_map/all_to_all | solution.py:82
  24.6 17.9 %copy-start.24 = (s32[4]{0:T(128)S(1)}, s32[4]{0:T(128)}, u32[]{:S(2)}) copy-start(s32[4]{0:T(128)} %param.14) | copy-start | bytes 52
  24.6 17.9 %copy-start.25 = (s32[4]{0:T(128)S(1)}, s32[4]{0:T(128)}, u32[]{:S(2)}) copy-start(s32[4]{0:T(128)} %param.15) | copy-start | bytes 52
  44.3 60.8 %all-to-all-start.2 = ((bf16[4,128,768]{2,1,0:T(8,128)(2,1)}), bf16[4,128,768]{2,1,0:T(8,128)(2,1)}, u32[]{:S(2)}, u32[]{:S(2)}) async-start(bf16[4,128,768]{2,1,0:T(8,128)(2,1)} %param.25), calls=%async_computation.2 | async-start | bytes 1572864 | tf_op jit(solution)/shard_map/all_to_all | solution.py:82
  49.3 197.3 %reduce-scatter.13.cloned.1.call-start = ((), (), s32[]{:S(2)}) async-start(), calls=%async_computation.13 | async-start | bytes 1327104 | tf_op jit(solution)/shard_map/reduce_scatter | solution.py:179
  54.7 16.7 %copy-start.2 = (bf16[512,768]{0,1:T(8,128)(2,1)}, bf16[512,768]{0,1:T(8,128)(2,1)S(1)}, u32[]{:S(2)}) copy-start(bf16[512,768]{0,1:T(8,128)(2,1)S(1)} %copy.79) | copy-start | bytes 2359300
  59.4 12.1 %copy-start.4 = (bf16[512,768]{0,1:T(8,128)(2,1)}, bf16[512,768]{0,1:T(8,128)(2,1)S(1)}, u32[]{:S(2)}) copy-start(bf16[512,768]{0,1:T(8,128)(2,1)S(1)} %copy.78) | copy-start | bytes 2359300
  71.4 15.8 %copy-start.17 = (bf16[512,768]{1,0:T(8,128)(2,1)S(1)}, bf16[512,768]{1,0:T(8,128)(2,1)}, u32[]{:S(2)}) copy-start(bf16[512,768]{1,0:T(8,128)(2,1)} %copy-done.16) | copy-start | bytes 2359300
  88.3 12.8 %copy-start.12 = (bf16[512,768]{0,1:T(8,128)(2,1)}, bf16[512,768]{0,1:T(8,128)(2,1)S(1)}, u32[]{:S(2)}) copy-start(bf16[512,768]{0,1:T(8,128)(2,1)S(1)} %copy.77) | copy-start | bytes 2359300
  103.9 15.7 %copy-start.8 = (f32[512,768]{1,0:T(8,128)}, f32[512,768]{1,0:T(8,128)S(1)}, u32[]{:S(2)}) copy-start(f32[512,768]{1,0:T(8,128)S(1)} %get-tuple-element.70) | copy-start | bytes 4718596
  105.1 14.5 %slice-start = ((s8[4718592]{0:T(1024)(128)(4,1)}), s8[4194304]{0:T(1024)(128)(4,1)S(1)}, s32[]{:S(2)}) async-start(s8[4718592]{0:T(1024)(128)(4,1)} %bitcast.155), calls=%async_computation.17 | async-start | bytes 8388608
  129.9 116.8 %reduce-scatter.11.cloned.1.call-start = ((), (), s32[]{:S(2)}) async-start(), calls=%async_computation.12 | async-start | bytes 1327104 | tf_op jit(solution)/shard_map/reduce_scatter | solution.py:179
  162.3 87.0 %reduce-scatter.7.cloned.1.call-start = ((), (), s32[]{:S(2)}) async-start(), calls=%async_computation.10 | async-start | bytes 1327104 | tf_op jit(solution)/shard_map/reduce_scatter | solution.py:179
  162.3 9.9 %copy-start.3 = (bf16[512,768]{0,1:T(8,128)(2,1)S(1)}, bf16[512,768]{0,1:T(8,128)(2,1)}, u32[]{:S(2)}) copy-start(bf16[512,768]{0,1:T(8,128)(2,1)} %copy-done.2) | copy-start | bytes 2359300
  177.7 112.4 %reduce-scatter.9.cloned.1.call-start = ((), (), s32[]{:S(2)}) async-start(), calls=%async_computation.11 | async-start | bytes 1327104 | tf_op jit(solution)/shard_map/reduce_scatter | solution.py:179
  185.8 161.5 %reduce-scatter.17.cloned.1.call-start = ((), (), s32[]{:S(2)}) async-start(), calls=%async_computation.15 | async-start | bytes 5308416 | tf_op jit(solution)/shard_map/reduce_scatter | solution.py:179
  194.4 210.5 %reduce-scatter.15.cloned.1.call-start = ((), (), s32[]{:S(2)}) async-start(), calls=%async_computation.14 | async-start | bytes 5308416 | tf_op jit(solution)/shard_map/reduce_scatter | solution.py:179
  225.3 179.7 %all-to-all-start.1 = ((bf16[4,2,49152]{2,1,0:T(2,128)(2,1)}), bf16[4,2,49152]{2,1,0:T(2,128)(2,1)}, u32[]{:S(2)}, u32[]{:S(2)}) async-start(bf16[4,2,49152]{2,1,0:T(2,128)(2,1)} %reshape.329), calls=%async_computation.1 | async-start | bytes 1572864 | tf_op jit(solution)/shard_map/all_to_all | solution.py:85
  230.5 268.3 %all-reduce.3.cloned.1.call-start = ((), (), s32[]{:S(2)}) async-start(), calls=%async_computation.16 | async-start | bytes 3538944 | tf_op jit(solution)/shard_map/psum | solution.py:180
  244.6 165.3 %copy-start.5 = (s32[64,4,8,128]{3,1,2,0:T(4,128)S(1)}, s32[64,4,8,128]{3,1,2,0:T(4,128)}, u32[]{:S(2)}) copy-start(s32[64,4,8,128]{3,1,2,0:T(4,128)} %copy.99) | copy-start | bytes 3145732
  244.6 165.3 %copy-start.6 = (s32[64,4,8,128]{3,1,2,0:T(4,128)S(1)}, s32[64,4,8,128]{3,1,2,0:T(4,128)}, u32[]{:S(2)}) copy-start(s32[64,4,8,128]{3,1,2,0:T(4,128)} %copy.98) | copy-start | bytes 3145732
  404.9 86.8 %all-to-all-start.3 = ((bf16[4,2,49152]{2,1,0:T(2,128)(2,1)}), bf16[4,2,49152]{2,1,0:T(2,128)(2,1)}, u32[]{:S(2)}, u32[]{:S(2)}) async-start(bf16[4,2,49152]{2,1,0:T(2,128)(2,1)} %reshape.331), calls=%async_computation.3 | async-start | bytes 1572864 | tf_op jit(solution)/shard_map/all_to_all | solution.py:85
  427.0 11.5 %copy-start.10 = (s32[262144]{0:T(1024)S(1)}, s32[262144]{0:T(1024)}, u32[]{:S(2)}) copy-start(s32[262144]{0:T(1024)} %fusion.35) | copy-start | bytes 3145732
  (16 other events, 58.5 us)
Sparse Core Ops, SparseCore 0:
  130.0 38.2 reduce-scatter.12
  171.9 36.7 reduce-scatter.10
  212.5 36.7 reduce-scatter.6
  253.3 36.7 reduce-scatter.8
  293.4 53.8 reduce-scatter.16
  351.0 53.8 reduce-scatter.14
  407.8 90.9 all-reduce.2

commit v2 on v1

v2 whole, which is shorter than its diff:
```python
from functools import partial

import jax
import jax.numpy as jnp
from jax import lax
from jax.experimental import pallas as pl
from jax.experimental.pallas import tpu as pltpu
from jax.sharding import PartitionSpec as P

EPS = 1e-06
NEG = -1000000000.0
LIMITS = (12, 16, 23, 32, 46, 64, 91)
HIGH = lax.Precision.HIGHEST
MESH = pl.DeviceIdType.MESH
BF = jnp.bfloat16
F32 = jnp.float32

GROUP = 8
LANES = 128
WIDE = 256
CHUNKS = 10
SLOTS = 3
CHUNK_ROWS = 768


def dot_nn(left, right):
    return jnp.dot(left, right, preferred_element_type=F32)


def dot_nt(left, right):
    return lax.dot_general(left, right, (((1,), (1,)), ((), ())), preferred_element_type=F32)


def dot_tn(left, right):
    return lax.dot_general(left, right, (((0,), (0,)), ((), ())), preferred_element_type=F32)


def buckets(relative):
    distance = jnp.abs(relative)
    far_bucket = 8 + sum(((distance >= thresh).astype(jnp.int32) for thresh in LIMITS))
    return jnp.where(relative > 0, 16, 0) + jnp.where(distance < 8, distance, far_bucket)


def loop(count, body):
    lax.fori_loop(0, count, lambda index, none: (body(index), none)[1], None)


def at(index, size):
    if isinstance(index, int):
        return pl.ds(index * size, size)
    return pl.ds(pl.multiple_of(index * size, size), size)


def layer_kernel(
    lo_count,
    hidden,
    cot,
    query_len,
    doc_len,
    wq_hbm,
    wk_hbm,
    wv_hbm,
    wo_hbm,
    w1_hbm,
    w2_hbm,
    gain1,
    gain2,
    table,
    layer_out,
    grad_in,
    shares,
    small_out,
    x_row,
    c_row,
    wq,
    wk,
    wv,
    wo,
    w1,
    w2,
    n1,
    q,
    k,
    v,
    probs,
    o,
    n2,
    turned,
    mid,
    acc_a,
    acc_b,
    z,
    du,
    bias,
    vec,
    sums,
    d_three,
    dsc,
    tacc,
    grads,
    r_core,
    r_first,
    r_second,
    z_end,
    z_mid,
    small,
    small_in,
    w_sem,
    own_sem,
    x_send,
    x_recv,
    c_send,
    c_recv,
    y_send,
    y_recv,
    i_send,
    i_recv,
    core_send,
    core_recv,
    first_send,
    first_recv,
    second_send,
    second_recv,
    end_send,
    end_recv,
    mid_send,
    mid_recv,
    back_send,
    back_recv,
    share_sem,
    small_send,
    small_recv,
):
    dp = lax.axis_index("dp")
    sq = lax.axis_index("seq")
    seq_count, block, width = hidden.shape
    length = x_row.shape[0]
    heads = table.shape[1]
    pairs = heads // 2
    head_group = WIDE // LANES
    row_share = width // GROUP
    parts = w1_hbm.shape[1] // (GROUP * LANES)
    part_cols = GROUP * LANES
    vec_len = vec.shape[1]

    high = dp // lo_count
    bit0 = lax.rem(high, 2)
    bit1 = lax.rem(high // 2, 2)
    bit2 = lax.rem(high // 4, 2)
    step1 = 2 * lo_count * (1 - 2 * bit1)
    step2 = 4 * lo_count * (1 - 2 * bit2)
    core_dev = (dp + lo_count * (1 - 2 * bit0), sq)
    first_dev = (dp + (1 - bit0) * step1 + bit0 * step2, sq)
    second_dev = (dp + bit0 * step1 + (1 - bit0) * step2, sq)
    first_bit = (1 - bit0) * bit1 + bit0 * bit2
    second_bit = (1 - bit0) * bit2 + bit0 * bit1
    pair_dev = (dp, sq + 1 - 2 * lax.rem(sq, 2))
    mid_dev = (dp, 3 - sq)
    is_end = jnp.logical_or(sq == 0, sq == seq_count - 1)
    is_mid = jnp.logical_not(is_end)
    row_devs = [lax.rem(sq + step, seq_count) for step in range(1, seq_count)]

    def remote(src, dst, send, recv, device):
        return pltpu.make_async_remote_copy(
            src_ref=src, dst_ref=dst, send_sem=send, recv_sem=recv, device_id=device, device_id_type=MESH
        )

    barrier = pltpu.get_barrier_semaphore()
    for device in [core_dev, first_dev, second_dev] + [(dp, other) for other in row_devs]:
        pl.semaphore_signal(barrier, inc=1, device_id=device, device_id_type=MESH)
    pl.semaphore_wait(barrier, 3 + len(row_devs))

    def deal(src_of, dst_of, send, recv):
        def copy(index):
            other = row_devs[index]
            return remote(src_of(other), dst_of(sq), send.at[index], recv.at[sq], (dp, other))

        def start():
            for index in range(len(row_devs)):
                copy(index).start()

        def arrived(other):
            remote(src_of(other), dst_of(other), send.at[0], recv.at[other], (dp, other)).wait_recv()

        def sent():
            for index in range(len(row_devs)):
                copy(index).wait_send()

        return start, arrived, sent

    x_start, x_arrived, x_sent = deal(
        lambda other: hidden.at[other], lambda src: x_row.at[at(src, block)], x_send, x_recv
    )
    c_start, c_arrived, c_sent = deal(
        lambda other: cot.at[other], lambda src: c_row.at[at(src, block)], c_send, c_recv
    )
    y_start, y_arrived, y_sent = deal(
        lambda other: z.at[at(other, block), pl.ds(0, width)], lambda src: layer_out.at[src], y_send, y_recv
    )
    i_start, i_arrived, i_sent = deal(
        lambda other: n2.at[at(other, block)], lambda src: grad_in.at[src], i_send, i_recv
    )
    own_x = pltpu.make_async_copy(hidden.at[sq], x_row.at[at(sq, block)], own_sem.at[0])
    own_c = pltpu.make_async_copy(cot.at[sq], c_row.at[at(sq, block)], own_sem.at[1])
    own_y = pltpu.make_async_copy(z.at[at(sq, block), pl.ds(0, width)], layer_out.at[sq], own_sem.at[2])
    own_i = pltpu.make_async_copy(n2.at[at(sq, block)], grad_in.at[sq], own_sem.at[3])

    x_start()
    own_x.start()
    square = [
        pltpu.make_async_copy(src, dst, w_sem.at[index])
        for index, (src, dst) in enumerate(((wq_hbm, wq), (wk_hbm, wk), (wv_hbm, wv), (wo_hbm, wo)))
    ]
    for copy in square:
        copy.start()

    def part_copies(part):
        slot = part % 2
        span = parts * LANES
        copies = []
        for share in range(GROUP):
            place = pl.ds(share * span + part * LANES, LANES)
            cols = pl.ds(share * LANES, LANES)
            copies.append(pltpu.make_async_copy(w1_hbm.at[:, place], w1.at[slot, :, cols], w_sem.at[4 + 2 * part]))
            copies.append(pltpu.make_async_copy(w2_hbm.at[place], w2.at[slot, cols], w_sem.at[5 + 2 * part]))
        return copies

    def part_wait(part):
        slot = part % 2
        pltpu.make_async_copy(w1.at[slot], w1.at[slot], w_sem.at[4 + 2 * part]).wait()
        pltpu.make_async_copy(w2.at[slot], w2.at[slot], w_sem.at[5 + 2 * part]).wait()

    for part in range(2):
        for copy in part_copies(part):
            copy.start()
    own_c.start()

    def rows_of(chunk):
        return CHUNK_ROWS if chunk < 2 * parts else 6 * row_share

    def piece(ref, *index):
        chunk = index[0]
        return ref.at[index + (slice(None),) * (len(ref.shape) - 2 - len(index)) + (pl.ds(0, rows_of(chunk)),)]

    def grad_half(chunk, side):
        return grads.at[chunk % SLOTS, side, :, :, pl.ds(0, rows_of(chunk))]

    def core_copy(chunk):
        return remote(
            grad_half(chunk, 1 - bit0), piece(r_core, chunk), core_send.at[chunk], core_recv.at[chunk], core_dev
        )

    def first_copy(chunk):
        return remote(
            piece(r_core, chunk, 1 - first_bit),
            piece(r_first, chunk),
            first_send.at[chunk],
            first_recv.at[chunk],
            first_dev,
        )

    def second_copy(chunk):
        return remote(
            piece(r_first, chunk, 1 - second_bit),
            piece(r_second, chunk),
            second_send.at[chunk],
            second_recv.at[chunk],
            second_dev,
        )

    def end_copy(chunk):
        return remote(
            piece(r_second, chunk), piece(z_end, chunk), end_send.at[chunk], end_recv.at[chunk], pair_dev
        )

    def mid_copy(chunk):
        return remote(
            piece(r_second, chunk), piece(z_mid, chunk), mid_send.at[chunk], mid_recv.at[chunk], mid_dev
        )

    def back_copy(chunk):
        return remote(
            piece(z_end, chunk), piece(shares, chunk), back_send.at[chunk], back_recv.at[chunk], pair_dev
        )

    def share_copy(chunk):
        return pltpu.make_async_copy(piece(z_end, chunk), piece(shares, chunk), share_sem.at[chunk])

    def core_done(chunk):
        copy = core_copy(chunk)
        copy.wait_recv()
        rows = pl.ds(0, rows_of(chunk))

        def add(index):
            one, two = index // 2, lax.rem(index, 2)
            r_core[chunk, one, two, rows] += grads[chunk % SLOTS, bit0, one, two, rows]

        loop(4, add)
        first_copy(chunk).start()
        copy.wait_send()

    def first_done(chunk):
        first_copy(chunk).wait_recv()
        rows = pl.ds(0, rows_of(chunk))

        def add(index):
            r_first[chunk, index, rows] += r_core[chunk, first_bit, index, rows]

        loop(2, add)
        second_copy(chunk).start()

    def second_done(chunk):
        second_copy(chunk).wait_recv()
        rows = pl.ds(0, rows_of(chunk))
        r_second[chunk, rows] += r_first[chunk, second_bit, rows]

        @pl.when(is_end)
        def _():
            end_copy(chunk).start()

    def end_done(chunk):
        rows = pl.ds(0, rows_of(chunk))

        @pl.when(is_mid)
        def _():
            end_copy(chunk).wait_recv()
            r_second[chunk, rows] += z_end[chunk, rows]
            mid_copy(chunk).start()

    def mid_done(chunk):
        rows = pl.ds(0, rows_of(chunk))

        @pl.when(is_mid)
        def _():
            mid_copy(chunk).wait_recv()
            z_end[chunk, rows] = r_second[chunk, rows] + z_mid[chunk, rows]
            back_copy(chunk).start()
            share_copy(chunk).start()

    def back_done(chunk):
        @pl.when(is_end)
        def _():
            back_copy(chunk).wait_recv()

    stages = (core_done, first_done, second_done, end_done, mid_done, back_done)

    def settle():
        for chunk in range(CHUNKS):
            first_copy(chunk).wait_send()
            second_copy(chunk).wait_send()

        @pl.when(is_end)
        def _():
            for chunk in range(CHUNKS):
                end_copy(chunk).wait_send()

        @pl.when(is_mid)
        def _():
            for chunk in range(CHUNKS):
                mid_copy(chunk).wait_send()
                back_copy(chunk).wait_send()
                share_copy(chunk).wait()

    def tick(spot):
        for stage, chunk in PLAN.get(spot, ()):
            stages[stage](chunk)

    def place_of(share):
        one, two, three = share % 2, (share // 2) % 2, share // 4
        return (one, two, three) if one == 0 else (one, three, two)

    distance = lax.broadcasted_iota(jnp.int32, (1, vec_len), 1) - vec_len // 2
    bucket_row = buckets(distance)
    bucket_count = table.shape[0]
    one_hot = (
        jnp.broadcast_to(bucket_row, (bucket_count, vec_len))
        == lax.broadcasted_iota(jnp.int32, (bucket_count, vec_len), 0)
    ).astype(F32)
    vec[pl.ds(0, heads), :] = dot_tn(table[...], one_hot.astype(BF))
    sub = lax.broadcasted_iota(jnp.int32, (8, vec_len), 0)

    def build_bias(head):
        rows = jnp.broadcast_to(vec[pl.ds(head, 1), :], (8, vec_len))
        for shift in (1, 2, 4):
            rows = jnp.where((sub & shift) != 0, pltpu.roll(rows, shift, 1), rows)
        shift = 8
        while shift < block:
            rows = jnp.concatenate([rows, pltpu.roll(rows, shift, 1)], axis=0)
            shift *= 2
        bias[head] = rows.astype(BF)

    loop(heads, build_bias)

    total_len = query_len[sq] + doc_len[sq]
    key_mask = jnp.where(
        lax.broadcasted_iota(jnp.int32, (1, length), 1) < total_len, jnp.float32(0), jnp.float32(NEG)
    )
    low_lanes = lax.broadcasted_iota(jnp.int32, (1, LANES), 1) < LANES // 2

    def half_of(values, half):
        keep = low_lanes if half == 0 else jnp.logical_not(low_lanes)
        return jnp.where(keep, values, jnp.zeros_like(values))

    gain_one = gain1[...].astype(F32)
    gain_two = gain2[...].astype(F32)

    own_x.wait()
    for other in row_devs:
        x_arrived(other)
    c_start()

    def norm_first(index):
        rows = at(index, block)
        values = x_row[rows, :].astype(F32)
        factor = lax.rsqrt(jnp.mean(values * values, axis=-1, keepdims=True) + EPS)
        n1[rows, :] = (values * factor * gain_one).astype(BF)

    loop(seq_count, norm_first)
    for copy in square:
        copy.wait()

    def project(index):
        cols = at(index, WIDE)
        q[:, cols] = dot_nn(n1[...], wq[:, cols]).astype(BF)
        k[:, cols] = dot_nn(n1[...], wk[:, cols]).astype(BF)
        v[:, cols] = dot_nn(n1[...], wv[:, cols]).astype(BF)

    loop(width // WIDE, project)

    def attend(pair):
        cols = at(pair, LANES)
        keys = k[:, cols]
        values = v[:, cols]
        for tile in range(length // WIDE):
            rows = pl.ds(tile * WIDE, WIDE)
            queries = q[rows, cols]
            total = None
            for half in range(2):
                head = 2 * pair + half
                scores = dot_nt(half_of(queries, half), keys)
                weights = []
                for part in range(WIDE // block):
                    start = vec_len // 2 - tile * WIDE - part * block
                    here = scores[part * block : (part + 1) * block]
                    here = here + bias[head, :, pl.ds(start, length)].astype(F32) + key_mask
                    here = jnp.exp(here - jnp.max(here, axis=-1, keepdims=True))
                    scale = 1.0 / jnp.sum(here, axis=-1, keepdims=True)
                    weights.append((here * scale).astype(BF))
                weights = jnp.concatenate(weights, axis=0)
                probs[head, rows, :] = weights
                term = dot_nn(weights, half_of(values, half))
                total = term if total is None else total + term
            o[rows, cols] = total.astype(BF)

    loop(pairs, attend)

    def attn_out(index):
        cols = at(index, WIDE)
        mid[:, cols] = x_row[:, cols].astype(F32) + dot_nn(o[...], wo[:, cols])

    loop(width // WIDE, attn_out)

    def norm_second(index):
        rows = at(index, block)
        values = mid[rows, :]
        factor = lax.rsqrt(jnp.mean(values * values, axis=-1, keepdims=True) + EPS)
        n2[rows, :] = (values * factor * gain_two).astype(BF)

    loop(seq_count, norm_second)

    def turn(source):
        def body(index):
            span = at(index, LANES)
            turned[span, :] = source[:, span].T

        loop(width // LANES, body)

    def put(chunk, values, row_of):
        for share in range(GROUP):
            for side in range(values.shape[1] // LANES):
                one, two, three = place_of(share)
                grads[chunk % SLOTS, one, two, three, pl.ds(row_of(side), row_share), :] = values[
                    share * row_share : (share + 1) * row_share, side * LANES : (side + 1) * LANES
                ].astype(BF)

    turn(n2)
    own_c.wait()
    for other in row_devs:
        c_arrived(other)

    for part in range(parts):
        slot = part % 2
        outer_chunk, inner_chunk = 2 * part, 2 * part + 1
        part_wait(part)

        def hidden_units(index):
            cols = at(index, WIDE)
            inner = dot_nn(n2[...], w1[slot, :, cols])
            back = dot_nt(c_row[...], w2[slot, cols, :])
            square_in = inner * inner
            bend = jnp.tanh(inner * (0.7978845608028654 + (0.7978845608028654 * 0.044715) * square_in))
            half_in = 0.5 * inner
            z[:, cols] = (half_in + half_in * bend).astype(BF)
            slope = 0.7978845608028654 + (3 * 0.7978845608028654 * 0.044715) * square_in
            slope = 0.5 + 0.5 * bend + half_in * (1 - bend * bend) * slope
            du[:, cols] = (back * slope).astype(BF)

        loop(part_cols // WIDE, hidden_units)
        tick(("units", part))

        def outer_tile(index):
            values = dot_tn(z[:, at(index, WIDE)], c_row[...])
            bit_one, bit_two = lax.rem(index, 2), index // 2
            for side in range(2):
                one, two = (bit_one, bit_two) if side == 0 else (bit_two, bit_one)
                for col in range(width // LANES):
                    grads[outer_chunk % SLOTS, side, one, two, pl.ds(col * LANES, LANES), :] = values[
                        side * LANES : (side + 1) * LANES, col * LANES : (col + 1) * LANES
                    ].astype(BF)

        loop(part_cols // WIDE, outer_tile)
        core_copy(outer_chunk).start()
        tick(("outer", part))

        def inner_tile(index):
            values = dot_nn(turned[...], du[:, at(index, WIDE)])
            put(inner_chunk, values, lambda side: pl.multiple_of((2 * index + side) * row_share, row_share))

        loop(part_cols // WIDE, inner_tile)
        core_copy(inner_chunk).start()
        tick(("inner", part))

        def add_up(index):
            cols = at(index, WIDE)
            term = dot_nn(z[...], w2[slot, :, cols])
            back = dot_nt(du[...], w1[slot, cols, :])
            if part == 0:
                acc_a[:, cols] = term
                acc_b[:, cols] = back
            else:
                acc_a[:, cols] += term
                acc_b[:, cols] += back

        loop(width // WIDE, add_up)
        if part + 2 < parts:
            for copy in part_copies(part + 2):
                copy.start()
        tick(("sums", part))

    sums[...] = jnp.zeros_like(sums)

    def back_second(index):
        rows = at(index, block)
        values = mid[rows, :]
        back = acc_b[rows, :]
        z[rows, pl.ds(0, width)] = (values + acc_a[rows, :]).astype(BF)
        factor = lax.rsqrt(jnp.mean(values * values, axis=-1, keepdims=True) + EPS)
        sums[1:2, :] += jnp.sum(back * values * factor, axis=0, keepdims=True)
        scaled = back * gain_two
        inside = jnp.mean(scaled * values, axis=-1, keepdims=True)
        total = c_row[rows, :].astype(F32) + factor * scaled - values * (factor * factor * factor * inside)
        acc_b[rows, :] = total
        n2[rows, :] = total.astype(BF)

    loop(seq_count, back_second)
    y_start()
    own_y.start()
    turn(o)
    attn_chunk = 2 * parts

    def attn_out_tile(index):
        cols = at(index, WIDE)
        values = dot_nn(turned[...], n2[:, cols])
        put(attn_chunk, values, lambda side: pl.multiple_of((2 * index + side) * row_share, row_share))
        c_row[:, cols] = dot_nt(n2[...], wo[cols, :]).astype(BF)

    loop(width // WIDE, attn_out_tile)
    core_copy(attn_chunk).start()
    turn(n1)
    tick(("attn_out", 0))

    def attend_back(group, inside):
        pair = group * head_group + inside
        cols = at(pair, LANES)
        keys = k[:, cols]
        values = v[:, cols]
        queries = q[:, cols]
        backs = c_row[:, cols]
        product = backs.astype(F32) * o[:, cols].astype(F32)
        for half in range(2):
            head = 2 * pair + half
            dot_sum = jnp.sum(half_of(product, half), axis=-1, keepdims=True)
            tacc[...] = jnp.zeros_like(tacc)
            for tile in range(length // WIDE):
                rows = pl.ds(tile * WIDE, WIDE)
                back = dot_nt(half_of(backs[tile * WIDE : (tile + 1) * WIDE], half), values)
                for part in range(WIDE // block):
                    base = tile * WIDE + part * block
                    start = vec_len // 2 - base
                    score = probs[head, pl.ds(base, block), :].astype(F32) * (
                        back[part * block : (part + 1) * block] - dot_sum[base : base + block]
                    )
                    tacc[:, pl.ds(start, length)] += score
                    dsc[half, pl.ds(base, block), :] = score.astype(BF)
            rows = tacc[...]
            size = block
            while size > 8:
                size //= 2
                rows = rows[:size] + pltpu.roll(rows[size:], vec_len - size, 1)
            for shift in (4, 2, 1):
                rows = jnp.where((sub & shift) != 0, pltpu.roll(rows, vec_len - shift, 1), rows)
            vec[pl.ds(head, 1), :] = jnp.sum(rows, axis=0, keepdims=True)
        out = at(inside, LANES)
        d_three[0, :, out] = (
            dot_nn(dsc[0], half_of(keys, 0)) + dot_nn(dsc[1], half_of(keys, 1))
        ).astype(BF)
        d_three[1, :, out] = (
            dot_tn(dsc[0], half_of(queries, 0)) + dot_tn(dsc[1], half_of(queries, 1))
        ).astype(BF)
        d_three[2, :, out] = (
            dot_tn(probs[2 * pair], half_of(backs, 0)) + dot_tn(probs[2 * pair + 1], half_of(backs, 1))
        ).astype(BF)

    for group in range(width // WIDE):
        chunk = attn_chunk + 1 + group
        for inside in range(head_group):
            attend_back(group, inside)
            tick(("heads", head_group * group + inside))

        def group_tile(index):
            values = dot_nn(turned[...], d_three[index])
            put(chunk, values, lambda side: pl.multiple_of((2 * index + side) * row_share, row_share))

        loop(3, group_tile)
        core_copy(chunk).start()
        cols = pl.ds(group * WIDE, WIDE)
        term = dot_nt(d_three[0], wq[:, cols]) + dot_nt(d_three[1], wk[:, cols]) + dot_nt(d_three[2], wv[:, cols])
        if group == 0:
            acc_a[...] = term
        else:
            acc_a[...] += term
        tick(("group", group))

    def back_first(index):
        rows = at(index, block)
        values = x_row[rows, :].astype(F32)
        back = acc_a[rows, :]
        factor = lax.rsqrt(jnp.mean(values * values, axis=-1, keepdims=True) + EPS)
        sums[0:1, :] += jnp.sum(back * values * factor, axis=0, keepdims=True)
        scaled = back * gain_one
        inside = jnp.mean(scaled * values, axis=-1, keepdims=True)
        total = acc_b[rows, :] + factor * scaled - values * (factor * factor * factor * inside)
        n2[rows, :] = total.astype(BF)

    loop(seq_count, back_first)
    table_sum = lax.dot_general(
        one_hot,
        vec[pl.ds(0, heads), :],
        (((1,), (1,)), ((), ())),
        precision=HIGH,
        preferred_element_type=F32,
    )
    small[0, pl.ds(0, 8), :] = sums[...]
    small[0, pl.ds(8, bucket_count), :] = jnp.zeros((bucket_count, width), F32)
    small[0, pl.ds(8, bucket_count), pl.ds(0, heads)] = table_sum

    def small_copy(step, device):
        return remote(small.at[step], small_in.at[step], small_send.at[step], small_recv.at[step], device)

    def small_step(step, device):
        copy = small_copy(step, device)
        copy.start()
        return copy

    copy = small_step(0, core_dev)
    i_start()
    own_i.start()
    copy.wait_recv()
    small[1] = small[0] + small_in[0]
    copy = small_step(1, (dp + step1, sq))
    copy.wait_recv()
    small[2] = small[1] + small_in[1]
    copy = small_step(2, (dp + step2, sq))
    copy.wait_recv()
    small[3] = small[2] + small_in[2]
    copy = small_step(3, pair_dev)
    copy.wait_recv()
    small[4] = small[3] + small_in[3]
    copy = small_step(4, (dp, lax.rem(sq + 2, 4)))
    copy.wait_recv()
    small_out[...] = small[4] + small_in[4]
    for step in range(5):
        small_copy(step, core_dev).wait_send()
    tick(("end", 0))
    settle()
    own_y.wait()
    own_i.wait()
    for other in row_devs:
        y_arrived(other)
        i_arrived(other)
    x_sent()
    c_sent()
    y_sent()
    i_sent()


def make_plan():
    spots = []
    for part in range(3):
        spots += [("units", part), ("outer", part), ("inner", part), ("sums", part)]
    spots.append(("attn_out", 0))
    for group in range(3):
        spots += [("heads", 2 * group), ("heads", 2 * group + 1), ("group", group)]
    spots.append(("end", 0))
    cost = {"units": 2.5, "outer": 1.5, "inner": 1.5, "sums": 2.0, "attn_out": 4.0, "heads": 3.0, "group": 2.0, "end": 4.0}
    made = {("outer", p): 2 * p for p in range(3)}
    made.update({("inner", p): 2 * p + 1 for p in range(3)})
    made.update({("attn_out", 0): 6, ("group", 0): 7, ("group", 1): 8, ("group", 2): 9})
    now, ready, plan = 0.0, {}, {}
    link = 0.0
    for spot in spots:
        now += cost[spot[0]]
        if spot in made:
            chunk = made[spot]
            core = now + 4.0
            link = max(link, core) + 6.5
            ready[chunk] = [core, link + 2.0, link + 6.0, link + 13.0, link + 19.0, link + 25.0]
        plan[spot] = []
        for chunk in sorted(ready):
            while ready[chunk] and (ready[chunk][0] <= now or spot[0] == "end"):
                if spot[0] == "end":
                    break
                ready[chunk].pop(0)
                plan[spot].append((5 - len(ready[chunk]), chunk))
    rest = []
    for chunk in sorted(ready):
        for left, when in enumerate(ready[chunk]):
            rest.append((when, 6 - len(ready[chunk]) + left, chunk))
    plan[("end", 0)] += [(stage, chunk) for when, stage, chunk in sorted(rest)]
    return plan


PLAN = make_plan()


def unpack_kernel(
    parts,
    row_share,
    shares,
    layer_in,
    grad_in_in,
    layer_out,
    grad_in,
    gq,
    gk,
    gv,
    go,
    gi,
    gf,
    sems,
):
    one = pltpu.make_async_copy(layer_in, layer_out, sems.at[0])
    two = pltpu.make_async_copy(grad_in_in, grad_in, sems.at[1])
    one.start()
    two.start()
    blocks = gq.shape[1] // LANES
    for part in range(parts):
        for col in range(blocks):
            gf[pl.ds(part * LANES, LANES), pl.ds(col * LANES, LANES)] = shares[
                2 * part, pl.ds(col * LANES, LANES), :
            ].astype(F32)
        for share in range(GROUP):
            gi[:, pl.ds((share * parts + part) * LANES, LANES)] = shares[
                2 * part + 1, pl.ds(share * row_share, row_share), :
            ].astype(F32)
    for col in range(blocks):
        go[:, pl.ds(col * LANES, LANES)] = shares[2 * parts, pl.ds(col * row_share, row_share), :].astype(F32)
    for group in range(blocks // 2):
        for index, ref in enumerate((gq, gk, gv)):
            for side in range(2):
                ref[:, pl.ds(group * WIDE + side * LANES, LANES)] = shares[
                    2 * parts + 1 + group, pl.ds((2 * index + side) * row_share, row_share), :
                ].astype(F32)
    one.wait()
    two.wait()


def on_device(
    dp_count,
    hidden_in,
    query_lengths,
    doc_lengths,
    w_query,
    w_key,
    w_value,
    w_attn_out,
    w_inner,
    w_outer,
    gain_attn,
    gain_ffn,
    bias_table,
    cotangent,
):
    rows, block, width = hidden_in.shape
    length = rows * block
    heads = bias_table.shape[1]
    ffn = w_inner.shape[1]
    part_cols = GROUP * LANES
    parts = ffn // part_cols
    vec_len = 2 * length
    lo_count = dp_count // GROUP
    row_share = width // GROUP

    def vm(*shape, dtype=BF):
        return pltpu.VMEM(shape, dtype)

    def dma(count):
        return pltpu.SemaphoreType.DMA((count,))

    hbm = pl.BlockSpec(memory_space=pl.ANY)
    vmem = pl.BlockSpec(memory_space=pltpu.VMEM)
    smem = pl.BlockSpec(memory_space=pltpu.SMEM)
    small_rows = 8 + bias_table.shape[0]
    layer_raw, grad_raw, shares, small = pl.pallas_call(
        partial(layer_kernel, lo_count),
        out_shape=(
            jax.ShapeDtypeStruct(hidden_in.shape, BF),
            jax.ShapeDtypeStruct(hidden_in.shape, BF),
            jax.ShapeDtypeStruct((CHUNKS, CHUNK_ROWS, LANES), BF),
            jax.ShapeDtypeStruct((small_rows, width), F32),
        ),
        in_specs=[hbm, hbm, smem, smem] + [hbm] * 6 + [vmem] * 3,
        out_specs=(hbm, hbm, hbm, vmem),
        scratch_shapes=[
            vm(length, width),
            vm(length, width),
            vm(width, width),
            vm(width, width),
            vm(width, width),
            vm(width, width),
            vm(2, width, part_cols),
            vm(2, part_cols, width),
            vm(length, width),
            vm(length, width),
            vm(length, width),
            vm(length, width),
            vm(heads, length, length),
            vm(length, width),
            vm(length, width),
            vm(width, length),
            vm(length, width, dtype=F32),
            vm(length, width, dtype=F32),
            vm(length, width, dtype=F32),
            vm(length, part_cols),
            vm(length, part_cols),
            vm(heads, block, vec_len),
            vm(16, vec_len, dtype=F32),
            vm(8, width, dtype=F32),
            vm(3, length, WIDE),
            vm(2, length, length),
            vm(block, vec_len, dtype=F32),
            vm(SLOTS, 2, 2, 2, CHUNK_ROWS, LANES),
            vm(CHUNKS, 2, 2, CHUNK_ROWS, LANES),
            vm(CHUNKS, 2, CHUNK_ROWS, LANES),
            vm(CHUNKS, CHUNK_ROWS, LANES),
            vm(CHUNKS, CHUNK_ROWS, LANES),
            vm(CHUNKS, CHUNK_ROWS, LANES),
            vm(5, small_rows, width, dtype=F32),
            vm(5, small_rows, width, dtype=F32),
            dma(4 + 2 * parts),
            dma(4),
        ]
        + [dma(rows)] * 8
        + [dma(CHUNKS)] * 13
        + [dma(5)] * 2,
        compiler_params=pltpu.CompilerParams(
            collective_id=0, has_side_effects=True, vmem_limit_bytes=64 * 2**20 - 2**19
        ),
    )(
        hidden_in,
        cotangent,
        query_lengths,
        doc_lengths,
        w_query,
        w_key,
        w_value,
        w_attn_out,
        w_inner,
        w_outer,
        gain_attn.reshape(1, width),
        gain_ffn.reshape(1, width),
        bias_table,
    )
    square = jax.ShapeDtypeStruct((row_share, width), F32)
    layer_out, grad_in, *grads = pl.pallas_call(
        partial(unpack_kernel, parts, row_share),
        out_shape=(
            jax.ShapeDtypeStruct(hidden_in.shape, BF),
            jax.ShapeDtypeStruct(hidden_in.shape, BF),
            square,
            square,
            square,
            square,
            jax.ShapeDtypeStruct((row_share, ffn), F32),
            jax.ShapeDtypeStruct((ffn // GROUP, width), F32),
        ),
        in_specs=[vmem, hbm, hbm],
        out_specs=(hbm, hbm) + (vmem,) * 6,
        scratch_shapes=[dma(2)],
        compiler_params=pltpu.CompilerParams(vmem_limit_bytes=32 * 2**20),
    )(shares, layer_raw, grad_raw)
    if lo_count > 1:
        high = lax.axis_index("dp") // lo_count

        def spread(part):
            whole = jnp.zeros((GROUP,) + part.shape, F32)
            whole = lax.dynamic_update_index_in_dim(whole, part, high, 0)
            whole = whole.reshape((GROUP * part.shape[0],) + part.shape[1:])
            return lax.psum_scatter(whole, "dp", scatter_dimension=0, tiled=True)

        grads = [spread(part) for part in grads]
        small = lax.psum(small, "dp") / GROUP
    gain_rows = width // dp_count
    gains = lax.dynamic_slice_in_dim(small[:2], lax.axis_index("dp") * gain_rows, gain_rows, axis=1)
    return (layer_out, grad_in, *grads, gains[0], gains[1], small[8:, :heads])


def solution(mesh):
    return jax.shard_map(
        partial(on_device, mesh.shape["dp"]),
        mesh=mesh,
        in_specs=(
            P("dp", "seq", None),
            P("dp"),
            P("dp"),
            P(),
            P(),
            P(),
            P(),
            P(),
            P(),
            P(),
            P(),
            P(),
            P("dp", "seq", None),
        ),
        out_specs=(
            P("dp", "seq", None),
            P("dp", "seq", None),
            P("dp", None),
            P("dp", None),
            P("dp", None),
            P("dp", None),
            P("dp", None),
            P("dp", None),
            P("dp"),
            P("dp"),
            P(),
        ),
        check_vma=False,
    )
```

time: 522 us -> 192 us (0.37)
  Pallas kernels: 0 us -> 180 us
  waiting for transfers between devices: 162 us -> 0 us
  matrix products: 141 us -> 0 us
  local copies, waits for them, and re-layouts: 74.5 us -> 10.4 us
  other arithmetic: 60.7 us -> 0 us
  blocking collectives: 41.1 us -> 0 us
  starting transfers between devices: 22.6 us -> 0 us
  between operations: 14.8 us -> 0.84 us
    pallas_call x0 -> x2, Pallas kernels: none -> 180 us  [the longest x1 177 us: on_device(): pl.pallas_call(partial(layer_kernel, lo_count), out_shape=(jax.ShapeDtype...]
    reduce_scatter x6 -> x0, waiting for transfers between devices: 158 us -> none  [share(): piece = lax.psum_scatter(part, 'dp', scatter_dimension=0, tiled=True)]
    dot_general x26 -> x0, matrix products: 141 us -> none  [the longest x6 24.4 us: outer_sum(): lax.dot_general(left, right, (((0,), (0,)), ((), ())), preferred_element_...]
    psum x1 -> x0, blocking collectives: 41.1 us -> none  [on_device(): small = lax.psum(small, ('dp', 'seq'))]
    unnamed x70 -> x8, local copies, waits for them, and re-layouts: 37.7 us -> 5.86 us
    convert_element_type x12 -> x0, other arithmetic: 23.8 us -> none  [the longest x6 10.9 us: share(): return lax.psum(piece, 'seq').astype(jnp.float32)]
    all_to_all x4 -> x0, starting transfers between devices: 21.6 us -> none  [the longest x2 11.6 us: to_rows(): lax.all_to_all(blocks, 'seq', split_axis=0, concat_axis=1, tiled=True)]
    dot_general x1 -> x0, local copies, waits for them, and re-layouts: 17.9 us -> none  [position_bias(): jnp.dot(one_hot, table_f, precision=HIGH)]
  transfers between devices with their start and end apart: 11 -> 0, of which waited for: 5 -> 0; matrix products, arithmetic and copies ran while one was open for 46% -> 0% of each run, Pallas kernels for 0% -> 0%
where the time goes in v2:
time: 192 us; the launch traced here: 191 us
  Pallas kernels  180 us (94%)
  local copies, waits for them, and re-layouts  10.4 us (5%)
    pallas_call x1, Pallas kernels, on_device(): pl.pallas_call(partial(layer_kernel, lo_count), out_shape=(jax.ShapeDtype...  177 us
    unnamed x8, local copies, waits for them, and re-layouts  5.86 us

profile of v2, /device:TPU:0, one launch (start us, length us, event | category | flops | bytes accessed | tf_op | source)
XLA Modules:
  0.0 191.2 jit_solution(8200363608034815714)
XLA Ops:
  0.6 1.3 reshape.28.gain1
  1.9 1.3 reshape.29.gain2
  3.2 1.4 copy.24.table
  4.5 176.9 %shard_map.212 = (bf16[4,128,768]{2,1,0:T(8,128)(2,1)}, bf16[4,128,768]{2,1,0:T(8,128)(2,1)}, bf16[10,768,128]{2,1,0:T(8,128)(2,1)}, f32[40,768]{1,0:T(8,128)}) custom-call(bf16[4,128,768]{2,1,0:T(8,128)(2,1)} %hidden.1, bf16[4,128,768]{2,1,0:T(8,128)(2,1)} %cot.1, s32[4]{0:T(128)} %query_len.1, s32[4]{0:T(128)} %doc_len.1, bf16[768,768]{1,0:T(8,128)(2,1)} %wq_hbm.1, ...), custom_call_target="tpu_custom_call" | custom-call | tf_op jit(solution)/shard_map/pallas_call | solution.py:824
  181.5 0.7 slice.12
  182.2 0.7 slice.15
  183.0 0.7 copy.25
  183.6 0.1 constant_dynamic-slice_fusion
  183.7 0.5 slice_bitcast_fusion
  184.2 0.0 copy-start
  184.2 1.5 copy-done
  185.8 0.0 copy-start.1
  185.8 1.1 copy-done.1
  186.9 0.0 copy-start.2
  186.9 1.1 copy-done.2
  188.0 2.9 %shard_map.213 = (bf16[4,128,768]{2,1,0:T(8,128)(2,1)}, bf16[4,128,768]{2,1,0:T(8,128)(2,1)}, f32[96,768]{1,0:T(8,128)}, f32[96,768]{1,0:T(8,128)}, f32[96,768]{...) custom-call(bf16[10,768,128]{2,1,0:T(8,128)(2,1)S(1)} %copy-done, ...), custom_call_target="tpu_custom_call" | custom-call | tf_op jit(solution)/shard_map/pallas_call | solution.py:895
Async XLA Ops:
  184.2 1.5 copy-start
  185.8 1.1 copy-start.1
  186.9 1.1 copy-start.2
